TPU v7x, 128 devices: a whole 4x4x4 slice. The times are simulated.
128 devices in a mesh: wide: 16 (over z, y), narrow: 8 (over x, core).
Axes of the slice: x: 4, y: 4, z: 4, core: 2. Of those that a mesh axis runs over, the one named last changes fastest.
Arguments:
- points: float32 [6, 1048576], P(None, ('wide', 'narrow')), may hold values from -6 to 6
- charges: float32 [16, 1048576], P(None, ('wide', 'narrow')), may hold values from -6 to 6
- leaf_skel: float32 [6, 524288], P(None, ('wide', 'narrow')), may hold values from -6 to 6
- node_skel: float32 [6, 8192], replicated, may hold values from -6 to 6
- group_skel: float32 [6, 1024], replicated, may hold values from -6 to 6
- source_basis: float32 [8192, 64, 128], P(('wide', 'narrow')), may hold values from -0.5 to 0.5
- target_basis: float32 [8192, 64, 128], P(('wide', 'narrow')), may hold values from -0.75 to 0.75
- leaf_upward: float32 [64, 524288], P(None, ('wide', 'narrow')), may hold values from -0.09375 to 0.09375
- leaf_downward: float32 [64, 524288], P(None, ('wide', 'narrow')), may hold values from -0.75 to 0.75
- node_upward: float32 [64, 8192], replicated, may hold values from -0.25 to 0.25
- node_downward: float32 [64, 8192], P(None, ('wide', 'narrow')), may hold values from -0.75 to 0.75
- near_list: int32 [8192, 8], P(('wide', 'narrow')), may hold values from -1 to 8191, as said below
- leaf_links: int32 [8192, 8], P(('wide', 'narrow')), may hold values from -1 to 8191, as said below
- node_links: int32 [128, 4], P(('wide', 'narrow')), may hold values from -1 to 127, as said below
- group_links: int32 [16, 8], P('wide'), may hold values from -1 to 15, as said below
Outputs:
- potential: float32 [16, 1048576], P(None, ('wide', 'narrow'))
Inputs may be any that keep to these rules, and one draw needn't show every extreme that they name: `near_list`: entry 0 of row l is l; the other used entries are distinct leaf clusters other than l within 64 of l; one device's rows hold at most 288 used entries together, exactly so many on every device but the first and the last. `leaf_links`: used entries of row l are distinct leaf clusters within 64 of l, none equal to l or to an entry of near_list row l. `node_links`: used entries of row d are distinct other nodes of the same group of 8 nodes. `group_links`: used entries of row g are distinct other groups.
All inputs are finite; a program needn't handle non-finite values.
Results may differ from a plain program's by a relative error of at most 0.0003.
Values sent between devices are 32-bit elements; how exact they have to be, the bound alone decides.
A program may use at most 64 MiB of HBM per device.

v0:
```python
import math

import jax
import jax.numpy as jnp
from jax import lax
from jax.sharding import PartitionSpec as P

PRECISE = lax.Precision.HIGHEST
SMOOTH = 0.25
COEFFICIENT = 1.0 / (4.0 * math.pi)


def with_halo(block, sides, width):
    for axis, dim in sides:
        count = lax.axis_size(axis)
        forward = [(i, i + 1) for i in range(count - 1)]
        backward = [(target, source) for source, target in forward]
        low = lax.ppermute(
            lax.slice_in_dim(block, block.shape[dim] - width, None, axis=dim), axis, forward
        )
        high = lax.ppermute(lax.slice_in_dim(block, 0, width, axis=dim), axis, backward)
        block = jnp.concatenate([low, block, high], axis=dim)
    return block


def double_layer(targets, sources):
    offset = targets[..., :, None] - sources[:3][..., None, :]
    distance = jnp.sum(offset * offset, axis=0) + SMOOTH
    flux_term = jnp.sum(offset * sources[3:6][..., None, :], axis=0)
    return flux_term * lax.rsqrt(distance) / distance * COEFFICIENT


def small_couple(target_points, source_points, source_values, links):
    usable = (links >= 0).astype(jnp.float32)
    sources = source_points[:, jnp.maximum(links, 0)]
    count = links.shape[0]
    targets = jnp.broadcast_to(target_points[:, None, :], (3, count, target_points.shape[1]))
    kernel = double_layer(targets, sources)
    weights = source_values * usable[:, None, None]
    return jnp.einsum("fqs,fts->qt", weights, kernel, precision=PRECISE)


def on_device(
    points,
    charges,
    leaf_skel,
    node_skel,
    group_skel,
    source_basis,
    target_basis,
    leaf_upward,
    leaf_downward,
    node_upward,
    node_downward,
    near_list,
    leaf_links,
    node_links,
    group_links,
):
    rhs_count = charges.shape[0]
    leaves = near_list.shape[0]
    slots = near_list.shape[1]
    leaf_size = points.shape[1] // leaves
    rank_size = source_basis.shape[1]
    group_size = lax.axis_size("narrow")
    group_count = lax.axis_size("wide")
    group_id = lax.axis_index("wide")
    node_id = group_id * group_size + lax.axis_index("narrow")
    first_leaf = node_id * leaves - leaves
    span_leaves = 3 * leaves
    rim_data = with_halo(
        jnp.concatenate([points, charges], axis=0), ((("wide", "narrow"), 1),), leaves * leaf_size
    )
    rim_cube = rim_data.reshape(6 + rhs_count, span_leaves, leaf_size)
    own_cube = points.reshape(6, leaves, leaf_size)
    near_local = jnp.clip(near_list - first_leaf, 0, span_leaves - 1)
    near_usable = (near_list >= 0).astype(jnp.float32)

    def near_block(start):
        leaf_ids = start + jnp.arange(8, dtype=jnp.int32)
        picked = near_local[leaf_ids]
        usable = near_usable[leaf_ids]
        sources = rim_cube[:, picked]
        targets = jnp.broadcast_to(own_cube[:3, leaf_ids][:, :, None, :], (3, 8, slots, leaf_size))
        kernel = double_layer(targets, sources[:6])
        weights = sources[6:] * usable[None, :, :, None]
        return jnp.einsum("qbns,bnts->qbt", weights, kernel, precision=PRECISE)

    near_starts = jnp.arange(leaves // 8, dtype=jnp.int32) * 8
    near_part = lax.map(near_block, near_starts)
    near_part = jnp.transpose(near_part, (1, 0, 2, 3)).reshape(rhs_count, leaves * leaf_size)
    leaf_charges = jnp.einsum(
        "qlp,lrp->qlr",
        charges.reshape(rhs_count, leaves, leaf_size),
        source_basis,
        precision=PRECISE,
    )
    charge_flat = leaf_charges.reshape(rhs_count, leaves * rank_size)
    node_charges = jnp.einsum("rk,qk->qr", leaf_upward, charge_flat, precision=PRECISE)
    skeleton_data = with_halo(
        jnp.concatenate([leaf_skel, charge_flat], axis=0),
        ((("wide", "narrow"), 1),),
        leaves * rank_size,
    )
    skeleton_cube = skeleton_data.reshape(6 + rhs_count, span_leaves, rank_size)
    leaf_cube = leaf_skel.reshape(6, leaves, rank_size)
    far_local = jnp.clip(leaf_links - first_leaf, 0, span_leaves - 1)
    far_usable = (leaf_links >= 0).astype(jnp.float32)
    far_slots = leaf_links.shape[1]

    def far_block(start):
        leaf_ids = start + jnp.arange(8, dtype=jnp.int32)
        picked = far_local[leaf_ids]
        usable = far_usable[leaf_ids]
        sources = skeleton_cube[:, picked]
        targets = jnp.broadcast_to(
            leaf_cube[:3, leaf_ids][:, :, None, :], (3, 8, far_slots, rank_size)
        )
        kernel = double_layer(targets, sources[:6])
        weights = sources[6:] * usable[None, :, :, None]
        return jnp.einsum("qbfs,bfts->qbt", weights, kernel, precision=PRECISE)

    far_starts = jnp.arange(leaves // 8, dtype=jnp.int32) * 8
    leaf_couple = lax.map(far_block, far_starts)
    leaf_couple = jnp.transpose(leaf_couple, (1, 0, 2, 3)).reshape(rhs_count, leaves, rank_size)
    upward_four = node_upward.reshape(rank_size, group_count, group_size, rank_size)
    own_nodes = lax.all_gather(node_charges[None], "narrow", axis=0, tiled=True)
    own_upward = lax.dynamic_index_in_dim(upward_four, group_id, 1, keepdims=False)
    own_group = jnp.einsum("rdk,dqk->qr", own_upward, own_nodes, precision=PRECISE)
    group_charges = lax.all_gather(own_group[None], "wide", axis=0, tiled=True)
    group_cube = group_skel.reshape(6, group_count, rank_size)
    group_ids = group_links[0]
    group_fields = small_couple(
        group_cube[:3, group_id], group_cube, group_charges[jnp.maximum(group_ids, 0)], group_ids
    )
    node_cube = node_skel.reshape(6, group_count * group_size, rank_size)
    node_ids = node_links[0]
    within = jnp.clip(node_ids - group_id * group_size, 0, group_size - 1)
    node_fields = jnp.dot(group_fields, node_downward, precision=PRECISE)
    node_fields = node_fields + small_couple(
        node_cube[:3, node_id], node_cube, own_nodes[within], node_ids
    )
    leaf_fields = jnp.dot(node_fields, leaf_downward, precision=PRECISE).reshape(
        rhs_count, leaves, rank_size
    )
    leaf_fields = leaf_fields + leaf_couple
    far_part = jnp.einsum("qlr,lrp->qlp", leaf_fields, target_basis, precision=PRECISE).reshape(
        rhs_count, leaves * leaf_size
    )
    return near_part + far_part


def solution(mesh):
    in_specs = (
        P(None, ("wide", "narrow")),
        P(None, ("wide", "narrow")),
        P(None, ("wide", "narrow")),
        P(),
        P(),
        P(("wide", "narrow"), None, None),
        P(("wide", "narrow"), None, None),
        P(None, ("wide", "narrow")),
        P(None, ("wide", "narrow")),
        P(),
        P(None, ("wide", "narrow")),
        P(("wide", "narrow"), None),
        P(("wide", "narrow"), None),
        P(("wide", "narrow"), None),
        P("wide", None),
    )
    out_specs = P(None, ("wide", "narrow"))
    return jax.shard_map(
        on_device, mesh=mesh, in_specs=in_specs, out_specs=out_specs, check_vma=False
    )
```

profile of v0, /device:TPU:0, one launch (start us, length us, event | category | flops | bytes accessed | tf_op | source)
XLA Modules:
  0.0 417.2 jit_solution(3982368309468552087)
XLA Ops:
  7.6 5.0 %convolution_bitcast_fusion.1 = f32[16,64,64]{2,0,1:T(8,128)S(1)} fusion(f32[64,64,128]{2,1,0:T(8,128)} %param.24, f32[16,8192]{1,0:T(8,128)} %param.20), kind=kOutput, calls=%fused_computation.62 | convolution fusion | flops 100663296 | bytes 2883584 | tf_op jit(solution)/shard_map/qlp,lrp->qlr/dot_general | solution.py:92
  28.8 17.3 %all-gather = f32[128,64]{1,0:T(8,128)S(1)} all-gather(f32[16,64]{1,0:T(8,128)S(1)} %fusion.76), channel_id=2, replica_groups=mesh['wide'=16,'narrow'=8] {'narrow'}, dimensions={0}, use_global_device_ids=true | all-gather | bytes 36864 | tf_op jit(solution)/shard_map/all_gather | solution.py:127
  46.1 4.6 %reshape.185 = f32[64,16,8,64]{3,2,1,0:T(8,128)} reshape(f32[64,8192]{1,0:T(8,128)} %param.28) | data formatting | bytes 4194304 | tf_op jit(solution)/shard_map/reshape | solution.py:126
  52.0 29.1 %all-gather.1 = f32[256,64]{1,0:T(8,128)S(1)} all-gather(f32[16,64]{1,0:T(8,128)S(1)} %convolution_bitcast_fusion.4), channel_id=3, replica_groups=mesh['wide'=16,'narrow'=8] {'wide'}, dimensions={0}, use_global_device_ids=true | all-gather | bytes 69632 | tf_op jit(solution)/shard_map/all_gather | solution.py:130
  93.8 4.3 %copy.128 = f32[22,192,64]{2,0,1:T(8,128)} copy(f32[22,192,64]{2,1,0:T(8,128)} %reshape.190) | data formatting | bytes 2162688 | tf_op jit(solution)/shard_map/while | solution.py:124
  98.1 120.8 %while.21 = (s32[]{:T(128)}, f32[8,16,8,64]{3,1,2,0:T(8,128)}, s32[8]{0:T(128)S(1)}, f32[6,64,64]{2,1,0:T(8,128)S(1)}, s32[64,8]{1,0:T(8,128)S(1)}, /*index=5*/f...) while((s32[]{:T(128)}, f32[8,16,8,64]{3,1,2,0:T(8,128)}, s32[8]{0:T(128)S(1)}, ...), condition=%wide.region_11.12_spmd, body=%wide.region_8.11_spmd.sunk | while | flops 54855920 | bytes 8127313 | solution.py:124
  103.2 4.3 %fusion.104 = (f32[8,8,64,64]{3,2,1,0:T(8,128)}, f32[8,8,64,64]{3,2,1,0:T(8,128)}) fusion(f32[3,8,8,64]{3,2,1,0:T(8,128)S(1)} %copy.163, f32[3,8,64]{2,1,0:T(8,128)S(1)} %bitcast.150, f32[3,8,8,64]{3,2,1,0:T(8,128)S(1)} %copy.164), kind=kLoop, calls=%fused_computation.39.clone.1 | loop fusion | flops 3407872 | bytes 2201600 | tf_op jit(solution)/shard_map/while/body/eval_jaxpr/reduce_sum | solution.py:28
  108.0 5.3 %fusion.105 = f32[8,16,8,64]{3,1,2,0:T(8,128)} fusion(f32[8,16,8,64]{3,1,2,0:T(8,128)} %get-tuple-element.321, s32[]{:T(128)S(6)} %copy.175, f32[8,8,64,64]{3,2,1,0:T(8,128)} %get-tuple-element.286, f32[8,8,64,64]{3,2,1,0:T(8,128)} %get-tuple-element.287, f32[22,8,8,64]{3,0,2,1:T(8,128)S(1)} %bitcast.142, f32[8,8]{1,0:T(8,128)S(1)} %gather_fusion.7), kind=kOutput, calls=%fused_computation.47.clone.1 | convolution fusion | flops 51445760 | bytes 4788228 | tf_op jit(solution)/shard_map/while/body/eval_jaxpr/qbfs,bfts->qbt/dot_general | solution.py:121
  123.1 5.3 %fusion.105 = f32[8,16,8,64]{3,1,2,0:T(8,128)} fusion(f32[8,16,8,64]{3,1,2,0:T(8,128)} %get-tuple-element.321, s32[]{:T(128)S(6)} %copy.175, f32[8,8,64,64]{3,2,1,0:T(8,128)} %get-tuple-element.286, f32[8,8,64,64]{3,2,1,0:T(8,128)} %get-tuple-element.287, f32[22,8,8,64]{3,0,2,1:T(8,128)S(1)} %bitcast.142, f32[8,8]{1,0:T(8,128)S(1)} %gather_fusion.7), kind=kOutput, calls=%fused_computation.47.clone.1 | convolution fusion | flops 51445760 | bytes 4788228 | tf_op jit(solution)/shard_map/while/body/eval_jaxpr/qbfs,bfts->qbt/dot_general | solution.py:121
  138.2 5.3 %fusion.105 = f32[8,16,8,64]{3,1,2,0:T(8,128)} fusion(f32[8,16,8,64]{3,1,2,0:T(8,128)} %get-tuple-element.321, s32[]{:T(128)S(6)} %copy.175, f32[8,8,64,64]{3,2,1,0:T(8,128)} %get-tuple-element.286, f32[8,8,64,64]{3,2,1,0:T(8,128)} %get-tuple-element.287, f32[22,8,8,64]{3,0,2,1:T(8,128)S(1)} %bitcast.142, f32[8,8]{1,0:T(8,128)S(1)} %gather_fusion.7), kind=kOutput, calls=%fused_computation.47.clone.1 | convolution fusion | flops 51445760 | bytes 4788228 | tf_op jit(solution)/shard_map/while/body/eval_jaxpr/qbfs,bfts->qbt/dot_general | solution.py:121
  153.2 5.3 %fusion.105 = f32[8,16,8,64]{3,1,2,0:T(8,128)} fusion(f32[8,16,8,64]{3,1,2,0:T(8,128)} %get-tuple-element.321, s32[]{:T(128)S(6)} %copy.175, f32[8,8,64,64]{3,2,1,0:T(8,128)} %get-tuple-element.286, f32[8,8,64,64]{3,2,1,0:T(8,128)} %get-tuple-element.287, f32[22,8,8,64]{3,0,2,1:T(8,128)S(1)} %bitcast.142, f32[8,8]{1,0:T(8,128)S(1)} %gather_fusion.7), kind=kOutput, calls=%fused_computation.47.clone.1 | convolution fusion | flops 51445760 | bytes 4788228 | tf_op jit(solution)/shard_map/while/body/eval_jaxpr/qbfs,bfts->qbt/dot_general | solution.py:121
  168.3 5.4 %fusion.105 = f32[8,16,8,64]{3,1,2,0:T(8,128)} fusion(f32[8,16,8,64]{3,1,2,0:T(8,128)} %get-tuple-element.321, s32[]{:T(128)S(6)} %copy.175, f32[8,8,64,64]{3,2,1,0:T(8,128)} %get-tuple-element.286, f32[8,8,64,64]{3,2,1,0:T(8,128)} %get-tuple-element.287, f32[22,8,8,64]{3,0,2,1:T(8,128)S(1)} %bitcast.142, f32[8,8]{1,0:T(8,128)S(1)} %gather_fusion.7), kind=kOutput, calls=%fused_computation.47.clone.1 | convolution fusion | flops 51445760 | bytes 4788228 | tf_op jit(solution)/shard_map/while/body/eval_jaxpr/qbfs,bfts->qbt/dot_general | solution.py:121
  183.4 5.3 %fusion.105 = f32[8,16,8,64]{3,1,2,0:T(8,128)} fusion(f32[8,16,8,64]{3,1,2,0:T(8,128)} %get-tuple-element.321, s32[]{:T(128)S(6)} %copy.175, f32[8,8,64,64]{3,2,1,0:T(8,128)} %get-tuple-element.286, f32[8,8,64,64]{3,2,1,0:T(8,128)} %get-tuple-element.287, f32[22,8,8,64]{3,0,2,1:T(8,128)S(1)} %bitcast.142, f32[8,8]{1,0:T(8,128)S(1)} %gather_fusion.7), kind=kOutput, calls=%fused_computation.47.clone.1 | convolution fusion | flops 51445760 | bytes 4788228 | tf_op jit(solution)/shard_map/while/body/eval_jaxpr/qbfs,bfts->qbt/dot_general | solution.py:121
  198.5 5.3 %fusion.105 = f32[8,16,8,64]{3,1,2,0:T(8,128)} fusion(f32[8,16,8,64]{3,1,2,0:T(8,128)} %get-tuple-element.321, s32[]{:T(128)S(6)} %copy.175, f32[8,8,64,64]{3,2,1,0:T(8,128)} %get-tuple-element.286, f32[8,8,64,64]{3,2,1,0:T(8,128)} %get-tuple-element.287, f32[22,8,8,64]{3,0,2,1:T(8,128)S(1)} %bitcast.142, f32[8,8]{1,0:T(8,128)S(1)} %gather_fusion.7), kind=kOutput, calls=%fused_computation.47.clone.1 | convolution fusion | flops 51445760 | bytes 4788228 | tf_op jit(solution)/shard_map/while/body/eval_jaxpr/qbfs,bfts->qbt/dot_general | solution.py:121
  213.5 5.4 %fusion.105 = f32[8,16,8,64]{3,1,2,0:T(8,128)} fusion(f32[8,16,8,64]{3,1,2,0:T(8,128)} %get-tuple-element.321, s32[]{:T(128)S(6)} %copy.175, f32[8,8,64,64]{3,2,1,0:T(8,128)} %get-tuple-element.286, f32[8,8,64,64]{3,2,1,0:T(8,128)} %get-tuple-element.287, f32[22,8,8,64]{3,0,2,1:T(8,128)S(1)} %bitcast.142, f32[8,8]{1,0:T(8,128)S(1)} %gather_fusion.7), kind=kOutput, calls=%fused_computation.47.clone.1 | convolution fusion | flops 51445760 | bytes 4788228 | tf_op jit(solution)/shard_map/while/body/eval_jaxpr/qbfs,bfts->qbt/dot_general | solution.py:121
  228.1 185.7 %while.20 = (s32[]{:T(128)}, f32[8,16,8,128]{3,1,2,0:T(8,128)}, s32[8]{0:T(128)S(1)}, f32[6,64,128]{2,1,0:T(8,128)S(1)}, s32[64,8]{1,0:T(8,128)S(1)}, /*index=5*...) while((s32[]{:T(128)}, f32[8,16,8,128]{3,1,2,0:T(8,128)}, s32[8]{0:T(128)S(1)}, ...), condition=%wide.region_3.4_spmd, body=%wide.region_0.3_spmd.sunk | while | flops 219285744 | bytes 19843920 | solution.py:90
  233.1 10.2 %fusion.100 = (f32[8,8,128,128]{3,2,1,0:T(8,128)}, f32[8,8,128,128]{3,2,1,0:T(8,128)}) fusion(f32[3,8,8,128]{3,2,1,0:T(8,128)S(1)} %copy.161, f32[3,8,128]{2,1,0:T(8,128)S(1)} %bitcast.151, f32[3,8,8,128]{3,2,1,0:T(8,128)S(1)} %copy.162), kind=kLoop, calls=%fused_computation.15.clone.1 | loop fusion | flops 13631488 | bytes 8597504 | tf_op jit(solution)/shard_map/while/body/eval_jaxpr/reduce_sum | solution.py:28
  243.9 7.6 %fusion.101 = f32[8,16,8,128]{3,1,2,0:T(8,128)} fusion(f32[8,16,8,128]{3,1,2,0:T(8,128)} %get-tuple-element.297, s32[]{:T(128)S(6)} %copy.169, f32[8,8,128,128]{3,2,1,0:T(8,128)} %get-tuple-element.273, f32[8,8,128,128]{3,2,1,0:T(8,128)} %get-tuple-element.274, f32[22,8,8,128]{3,0,2,1:T(8,128)S(1)} %bitcast.144, f32[8,8]{1,0:T(8,128)S(1)} %gather_fusion.3), kind=kOutput, calls=%fused_computation.25.clone.1 | convolution fusion | flops 205651968 | bytes 8982532 | tf_op jit(solution)/shard_map/while/body/eval_jaxpr/qbns,bnts->qbt/dot_general | solution.py:87
  256.3 10.2 %fusion.100 = (f32[8,8,128,128]{3,2,1,0:T(8,128)}, f32[8,8,128,128]{3,2,1,0:T(8,128)}) fusion(f32[3,8,8,128]{3,2,1,0:T(8,128)S(1)} %copy.161, f32[3,8,128]{2,1,0:T(8,128)S(1)} %bitcast.151, f32[3,8,8,128]{3,2,1,0:T(8,128)S(1)} %copy.162), kind=kLoop, calls=%fused_computation.15.clone.1 | loop fusion | flops 13631488 | bytes 8597504 | tf_op jit(solution)/shard_map/while/body/eval_jaxpr/reduce_sum | solution.py:28
  267.1 7.6 %fusion.101 = f32[8,16,8,128]{3,1,2,0:T(8,128)} fusion(f32[8,16,8,128]{3,1,2,0:T(8,128)} %get-tuple-element.297, s32[]{:T(128)S(6)} %copy.169, f32[8,8,128,128]{3,2,1,0:T(8,128)} %get-tuple-element.273, f32[8,8,128,128]{3,2,1,0:T(8,128)} %get-tuple-element.274, f32[22,8,8,128]{3,0,2,1:T(8,128)S(1)} %bitcast.144, f32[8,8]{1,0:T(8,128)S(1)} %gather_fusion.3), kind=kOutput, calls=%fused_computation.25.clone.1 | convolution fusion | flops 205651968 | bytes 8982532 | tf_op jit(solution)/shard_map/while/body/eval_jaxpr/qbns,bnts->qbt/dot_general | solution.py:87
  279.5 10.2 %fusion.100 = (f32[8,8,128,128]{3,2,1,0:T(8,128)}, f32[8,8,128,128]{3,2,1,0:T(8,128)}) fusion(f32[3,8,8,128]{3,2,1,0:T(8,128)S(1)} %copy.161, f32[3,8,128]{2,1,0:T(8,128)S(1)} %bitcast.151, f32[3,8,8,128]{3,2,1,0:T(8,128)S(1)} %copy.162), kind=kLoop, calls=%fused_computation.15.clone.1 | loop fusion | flops 13631488 | bytes 8597504 | tf_op jit(solution)/shard_map/while/body/eval_jaxpr/reduce_sum | solution.py:28
  290.3 7.6 %fusion.101 = f32[8,16,8,128]{3,1,2,0:T(8,128)} fusion(f32[8,16,8,128]{3,1,2,0:T(8,128)} %get-tuple-element.297, s32[]{:T(128)S(6)} %copy.169, f32[8,8,128,128]{3,2,1,0:T(8,128)} %get-tuple-element.273, f32[8,8,128,128]{3,2,1,0:T(8,128)} %get-tuple-element.274, f32[22,8,8,128]{3,0,2,1:T(8,128)S(1)} %bitcast.144, f32[8,8]{1,0:T(8,128)S(1)} %gather_fusion.3), kind=kOutput, calls=%fused_computation.25.clone.1 | convolution fusion | flops 205651968 | bytes 8982532 | tf_op jit(solution)/shard_map/while/body/eval_jaxpr/qbns,bnts->qbt/dot_general | solution.py:87
  302.7 10.2 %fusion.100 = (f32[8,8,128,128]{3,2,1,0:T(8,128)}, f32[8,8,128,128]{3,2,1,0:T(8,128)}) fusion(f32[3,8,8,128]{3,2,1,0:T(8,128)S(1)} %copy.161, f32[3,8,128]{2,1,0:T(8,128)S(1)} %bitcast.151, f32[3,8,8,128]{3,2,1,0:T(8,128)S(1)} %copy.162), kind=kLoop, calls=%fused_computation.15.clone.1 | loop fusion | flops 13631488 | bytes 8597504 | tf_op jit(solution)/shard_map/while/body/eval_jaxpr/reduce_sum | solution.py:28
  313.5 7.6 %fusion.101 = f32[8,16,8,128]{3,1,2,0:T(8,128)} fusion(f32[8,16,8,128]{3,1,2,0:T(8,128)} %get-tuple-element.297, s32[]{:T(128)S(6)} %copy.169, f32[8,8,128,128]{3,2,1,0:T(8,128)} %get-tuple-element.273, f32[8,8,128,128]{3,2,1,0:T(8,128)} %get-tuple-element.274, f32[22,8,8,128]{3,0,2,1:T(8,128)S(1)} %bitcast.144, f32[8,8]{1,0:T(8,128)S(1)} %gather_fusion.3), kind=kOutput, calls=%fused_computation.25.clone.1 | convolution fusion | flops 205651968 | bytes 8982532 | tf_op jit(solution)/shard_map/while/body/eval_jaxpr/qbns,bnts->qbt/dot_general | solution.py:87
  325.9 10.2 %fusion.100 = (f32[8,8,128,128]{3,2,1,0:T(8,128)}, f32[8,8,128,128]{3,2,1,0:T(8,128)}) fusion(f32[3,8,8,128]{3,2,1,0:T(8,128)S(1)} %copy.161, f32[3,8,128]{2,1,0:T(8,128)S(1)} %bitcast.151, f32[3,8,8,128]{3,2,1,0:T(8,128)S(1)} %copy.162), kind=kLoop, calls=%fused_computation.15.clone.1 | loop fusion | flops 13631488 | bytes 8597504 | tf_op jit(solution)/shard_map/while/body/eval_jaxpr/reduce_sum | solution.py:28
  336.6 7.6 %fusion.101 = f32[8,16,8,128]{3,1,2,0:T(8,128)} fusion(f32[8,16,8,128]{3,1,2,0:T(8,128)} %get-tuple-element.297, s32[]{:T(128)S(6)} %copy.169, f32[8,8,128,128]{3,2,1,0:T(8,128)} %get-tuple-element.273, f32[8,8,128,128]{3,2,1,0:T(8,128)} %get-tuple-element.274, f32[22,8,8,128]{3,0,2,1:T(8,128)S(1)} %bitcast.144, f32[8,8]{1,0:T(8,128)S(1)} %gather_fusion.3), kind=kOutput, calls=%fused_computation.25.clone.1 | convolution fusion | flops 205651968 | bytes 8982532 | tf_op jit(solution)/shard_map/while/body/eval_jaxpr/qbns,bnts->qbt/dot_general | solution.py:87
  349.0 10.2 %fusion.100 = (f32[8,8,128,128]{3,2,1,0:T(8,128)}, f32[8,8,128,128]{3,2,1,0:T(8,128)}) fusion(f32[3,8,8,128]{3,2,1,0:T(8,128)S(1)} %copy.161, f32[3,8,128]{2,1,0:T(8,128)S(1)} %bitcast.151, f32[3,8,8,128]{3,2,1,0:T(8,128)S(1)} %copy.162), kind=kLoop, calls=%fused_computation.15.clone.1 | loop fusion | flops 13631488 | bytes 8597504 | tf_op jit(solution)/shard_map/while/body/eval_jaxpr/reduce_sum | solution.py:28
  359.8 7.6 %fusion.101 = f32[8,16,8,128]{3,1,2,0:T(8,128)} fusion(f32[8,16,8,128]{3,1,2,0:T(8,128)} %get-tuple-element.297, s32[]{:T(128)S(6)} %copy.169, f32[8,8,128,128]{3,2,1,0:T(8,128)} %get-tuple-element.273, f32[8,8,128,128]{3,2,1,0:T(8,128)} %get-tuple-element.274, f32[22,8,8,128]{3,0,2,1:T(8,128)S(1)} %bitcast.144, f32[8,8]{1,0:T(8,128)S(1)} %gather_fusion.3), kind=kOutput, calls=%fused_computation.25.clone.1 | convolution fusion | flops 205651968 | bytes 8982532 | tf_op jit(solution)/shard_map/while/body/eval_jaxpr/qbns,bnts->qbt/dot_general | solution.py:87
  372.2 10.2 %fusion.100 = (f32[8,8,128,128]{3,2,1,0:T(8,128)}, f32[8,8,128,128]{3,2,1,0:T(8,128)}) fusion(f32[3,8,8,128]{3,2,1,0:T(8,128)S(1)} %copy.161, f32[3,8,128]{2,1,0:T(8,128)S(1)} %bitcast.151, f32[3,8,8,128]{3,2,1,0:T(8,128)S(1)} %copy.162), kind=kLoop, calls=%fused_computation.15.clone.1 | loop fusion | flops 13631488 | bytes 8597504 | tf_op jit(solution)/shard_map/while/body/eval_jaxpr/reduce_sum | solution.py:28
  383.0 7.6 %fusion.101 = f32[8,16,8,128]{3,1,2,0:T(8,128)} fusion(f32[8,16,8,128]{3,1,2,0:T(8,128)} %get-tuple-element.297, s32[]{:T(128)S(6)} %copy.169, f32[8,8,128,128]{3,2,1,0:T(8,128)} %get-tuple-element.273, f32[8,8,128,128]{3,2,1,0:T(8,128)} %get-tuple-element.274, f32[22,8,8,128]{3,0,2,1:T(8,128)S(1)} %bitcast.144, f32[8,8]{1,0:T(8,128)S(1)} %gather_fusion.3), kind=kOutput, calls=%fused_computation.25.clone.1 | convolution fusion | flops 205651968 | bytes 8982532 | tf_op jit(solution)/shard_map/while/body/eval_jaxpr/qbns,bnts->qbt/dot_general | solution.py:87
  395.4 10.2 %fusion.100 = (f32[8,8,128,128]{3,2,1,0:T(8,128)}, f32[8,8,128,128]{3,2,1,0:T(8,128)}) fusion(f32[3,8,8,128]{3,2,1,0:T(8,128)S(1)} %copy.161, f32[3,8,128]{2,1,0:T(8,128)S(1)} %bitcast.151, f32[3,8,8,128]{3,2,1,0:T(8,128)S(1)} %copy.162), kind=kLoop, calls=%fused_computation.15.clone.1 | loop fusion | flops 13631488 | bytes 8597504 | tf_op jit(solution)/shard_map/while/body/eval_jaxpr/reduce_sum | solution.py:28
  406.2 7.6 %fusion.101 = f32[8,16,8,128]{3,1,2,0:T(8,128)} fusion(f32[8,16,8,128]{3,1,2,0:T(8,128)} %get-tuple-element.297, s32[]{:T(128)S(6)} %copy.169, f32[8,8,128,128]{3,2,1,0:T(8,128)} %get-tuple-element.273, f32[8,8,128,128]{3,2,1,0:T(8,128)} %get-tuple-element.274, f32[22,8,8,128]{3,0,2,1:T(8,128)S(1)} %bitcast.144, f32[8,8]{1,0:T(8,128)S(1)} %gather_fusion.3), kind=kOutput, calls=%fused_computation.25.clone.1 | convolution fusion | flops 205651968 | bytes 8982532 | tf_op jit(solution)/shard_map/while/body/eval_jaxpr/qbns,bnts->qbt/dot_general | solution.py:87
  (322 shorter events, 165.3 us)
Async XLA Ops:
  0.0 220.5 %copy-start = (f32[64,64,128]{2,1,0:T(8,128)S(1)}, f32[64,64,128]{2,1,0:T(8,128)}, u32[]{:S(2)}) copy-start(f32[64,64,128]{2,1,0:T(8,128)} %param.25) | copy-start | bytes 6291460
  2.2 10.8 %copy-start.10 = (f32[6,4096]{1,0:T(8,128)S(1)}, f32[6,4096]{1,0:T(8,128)}, u32[]{:S(2)}) copy-start(f32[6,4096]{1,0:T(8,128)} %param.21) | copy-start | bytes 294916
  2.2 17.4 %copy-start.14 = (s32[64,8]{0,1:T(8,128)S(1)}, s32[64,8]{0,1:T(8,128)}, u32[]{:S(2)}) copy-start(s32[64,8]{0,1:T(8,128)} %param.30) | copy-start | bytes 6148
  2.2 17.4 %copy-start.15 = (s32[64,8]{0,1:T(8,128)S(1)}, s32[64,8]{0,1:T(8,128)}, u32[]{:S(2)}) copy-start(s32[64,8]{0,1:T(8,128)} %param.31) | copy-start | bytes 6148
  2.2 17.5 %copy-start.16 = (s32[1,8]{1,0:T(1,128)S(1)}, s32[1,8]{1,0:T(1,128)}, u32[]{:S(2)}) copy-start(s32[1,8]{1,0:T(1,128)} %param.33) | copy-start | bytes 100
  2.2 18.0 %copy-start.17 = (s32[1,4]{1,0:T(1,128)S(1)}, s32[1,4]{1,0:T(1,128)}, u32[]{:S(2)}) copy-start(s32[1,4]{1,0:T(1,128)} %param.32) | copy-start | bytes 52
  2.3 19.6 %copy-start.4 = (f32[6,8192]{1,0:T(8,128)S(1)}, f32[6,8192]{1,0:T(8,128)}, u32[]{:S(2)}) copy-start(f32[6,8192]{1,0:T(8,128)} %param.19) | copy-start | bytes 589828
  2.3 220.9 %collective-permute-start.1 = (f32[22,8192]{1,0:T(8,128)}, f32[22,8192]{1,0:T(8,128)}, u32[]{:S(2)}, u32[]{:S(2)}) collective-permute-start(f32[22,8192]{1,0:T(8,128)} %pad_maximum_fusion.2), channel_id=1, source_target_pairs={{1,0},{2,1},{3,2},{4,3},{5,4},{6,5},{7,6},{8,7},{9,8},{10,9},{11,1... | collective-permute-start | bytes 2162696 | tf_op jit(solution)/shard_map/ppermute | solution.py:21
  3.7 219.5 %collective-permute-start = (f32[22,8192]{1,0:T(8,128)}, f32[22,8192]{1,0:T(8,128)}, u32[]{:S(2)}, u32[]{:S(2)}) collective-permute-start(f32[22,8192]{1,0:T(8,128)} %pad_maximum_fusion.2), channel_id=1, source_target_pairs={{0,1},{1,2},{2,3},{3,4},{4,5},{5,6},{6,7},{7,8},{8,9},{9,10},{10,1... | collective-permute-start | bytes 2162696 | tf_op jit(solution)/shard_map/ppermute | solution.py:18
  12.6 12.7 %copy-start.13 = (f32[6,1024]{1,0:T(8,128)S(1)}, f32[6,1024]{1,0:T(8,128)}, u32[]{:S(2)}) copy-start(f32[6,1024]{1,0:T(8,128)} %param.23) | copy-start | bytes 73732
  13.8 76.5 %collective-permute-start.3 = (f32[22,4096]{1,0:T(8,128)}, f32[22,4096]{1,0:T(8,128)}, u32[]{:S(2)}, u32[]{:S(2)}) collective-permute-start(f32[22,4096]{1,0:T(8,128)} %pad_maximum_fusion.3), channel_id=1, source_target_pairs={{1,0},{2,1},{3,2},{4,3},{5,4},{6,5},{7,6},{8,7},{9,8},{10,9},{11,1... | collective-permute-start | bytes 1081352 | tf_op jit(solution)/shard_map/ppermute | solution.py:21
  15.1 75.2 %collective-permute-start.2 = (f32[22,4096]{1,0:T(8,128)}, f32[22,4096]{1,0:T(8,128)}, u32[]{:S(2)}, u32[]{:S(2)}) collective-permute-start(f32[22,4096]{1,0:T(8,128)} %pad_maximum_fusion.3), channel_id=1, source_target_pairs={{0,1},{1,2},{2,3},{3,4},{4,5},{5,6},{6,7},{7,8},{8,9},{9,10},{10,1... | collective-permute-start | bytes 1081352 | tf_op jit(solution)/shard_map/ppermute | solution.py:18
  46.1 35.5 %copy-start.12 = (f32[6,8192]{1,0:T(8,128)S(1)}, f32[6,8192]{1,0:T(8,128)}, u32[]{:S(2)}) copy-start(f32[6,8192]{1,0:T(8,128)} %param.22) | copy-start | bytes 589828
  84.5 4.1 copy-start.11
  93.8 4.3 %copy-start.3 = (f32[6,64,64]{2,1,0:T(8,128)S(1)}, f32[6,64,64]{2,1,0:T(8,128)}, u32[]{:S(2)}) copy-start(f32[6,64,64]{2,1,0:T(8,128)} %reshape.189) | copy-start | bytes 294916
  93.8 4.3 %copy-start.8 = (s32[64,8]{1,0:T(8,128)S(1)}, s32[64,8]{1,0:T(8,128)}, u32[]{:S(2)}) copy-start(s32[64,8]{1,0:T(8,128)} %copy.127) | copy-start | bytes 6148
  93.8 4.3 %copy-start.9 = (f32[64,8]{1,0:T(8,128)S(1)}, f32[64,8]{1,0:T(8,128)}, u32[]{:S(2)}) copy-start(f32[64,8]{1,0:T(8,128)} %copy.129) | copy-start | bytes 6148
  218.9 4.3 %copy-start.1 = (f32[16,8192]{1,0:T(8,128)S(1)}, f32[16,8192]{1,0:T(8,128)}, u32[]{:S(2)}) copy-start(f32[16,8192]{1,0:T(8,128)} %param.20) | copy-start | bytes 1572868
  218.9 4.3 %copy-start.5 = (f32[6,8192]{1,0:T(8,128)S(1)}, f32[6,8192]{1,0:T(8,128)}, u32[]{:S(2)}) copy-start(f32[6,8192]{1,0:T(8,128)} %param.19) | copy-start | bytes 589828
  225.4 2.7 copy-start.2
  225.4 2.7 copy-start.6
  225.4 2.7 copy-start.7
where the time goes:
time: 419 us; the launch traced here: 417 us
  other arithmetic  140 us (33%)
  matrix products  117 us (28%)
  local copies, waits for them, and re-layouts  101 us (24%)
  blocking collectives  46.3 us (11%)
  starting transfers between devices  10.4 us (2%)
    reduce_sum x18, other arithmetic, double_layer(): distance = jnp.sum(offset * offset, axis=0) + SMOOTH  117 us
    dot_general x8, matrix products, near_block(): return jnp.einsum('qbns,bnts->qbt', weights, kernel, precision=PRECISE)  61 us
    dot_general x8, matrix products, far_block(): return jnp.einsum('qbfs,bfts->qbt', weights, kernel, precision=PRECISE)  42.8 us
    all_gather x1, blocking collectives, on_device(): group_charges = lax.all_gather(own_group[None], 'wide', axis=0, tiled=True)  29.1 us
    gather x8, local copies, waits for them, and re-layouts, far_block(): sources = skeleton_cube[:, picked]  18.1 us
    gather x8, local copies, waits for them, and re-layouts, near_block(): sources = rim_cube[:, picked]  18.1 us
    all_gather x1, blocking collectives, on_device(): own_nodes = lax.all_gather(node_charges[None], 'narrow', axis=0, tiled=True)  17.3 us
    dynamic_slice x16, local copies, waits for them, and re-layouts, on_device(): near_part = lax.map(near_block, near_starts)  9.89 us
  transfers between devices with their start and end apart: 4, of which 0 were waited for; matrix products, arithmetic and copies ran while one was open for 39% of the time, Pallas kernels for 0%

commit v1 on v0

v1 whole, which is shorter than its diff:
```python
import functools
import math

import jax
import jax.numpy as jnp
from jax import lax
from jax.experimental import pallas as pl
from jax.experimental.pallas import tpu as pltpu
from jax.sharding import PartitionSpec as P

MESH = pl.DeviceIdType.MESH
HIGH = lax.Precision.HIGHEST
F32, BF16 = jnp.float32, jnp.bfloat16
SMOOTH = 0.25
COEFFICIENT = 1.0 / (4.0 * math.pi)
NT = (((1,), (1,)), ((), ()))
NN = (((1,), (0,)), ((), ()))
NEAR_PAIRS = 288
NEAR_STEP = 16
VMEM_LIMIT = 56 * 2**20


def dot(a, b, dims, precision=None):
    return lax.dot_general(a, b, dims, precision=precision, preferred_element_type=F32)


def halves(x):
    high = x.astype(BF16)
    return high, (x - high.astype(F32)).astype(BF16)


def twice(x):
    high, low = halves(x)
    stacked = jnp.concatenate([high, low], axis=0)
    return jnp.concatenate([stacked, stacked], axis=1)


def beside(x):
    high, low = halves(x)
    return jnp.concatenate([high, low], axis=1)


def pieces(x):
    first = x.astype(BF16).astype(F32)
    rest = x - first
    second = rest.astype(BF16).astype(F32)
    return first, second, rest - second


def lane(shape):
    return lax.broadcasted_iota(jnp.int32, shape, 1)


def row(shape):
    return lax.broadcasted_iota(jnp.int32, shape, 0)


def in_pairs(ref, count):
    return [
        ref[2 * i] + pltpu.roll(ref[2 * i + 1], 64, 1) for i in range(count // 2)
    ]


def exchange(
    points,
    charges,
    leaf_skel,
    source_basis,
    leaf_upward,
    node_upward,
    points_low,
    points_high,
    charges_low,
    charges_high,
    skel_low,
    skel_high,
    leaf_low,
    leaf_high,
    leaf_charges,
    nodes_out,
    groups_out,
    basis,
    own_upward,
    nodes,
    groups,
    node_mine,
    group_mine,
    load_sem,
    halo_send,
    halo_recv,
    node_send,
    node_recv,
    group_send,
    group_recv,
):
    n_wide, n_narrow = lax.axis_size("wide"), lax.axis_size("narrow")
    g, n = lax.axis_index("wide"), lax.axis_index("narrow")
    at_end = (n == n_narrow - 1).astype(jnp.int32)
    at_start = (n == 0).astype(jnp.int32)
    after = (lax.rem(g + at_end, n_wide), lax.rem(n + 1, n_narrow))
    before = (
        lax.rem(g - at_start + n_wide, n_wide),
        lax.rem(n - 1 + n_narrow, n_narrow),
    )

    load_basis = pltpu.make_async_copy(source_basis, basis, load_sem.at[0])
    load_basis.start()
    load_upward = pltpu.make_async_copy(
        node_upward.at[:, pl.ds(pl.multiple_of(g * (64 * n_narrow), 128), 64 * n_narrow)],
        own_upward,
        load_sem.at[1],
    )
    load_upward.start()

    barrier = pltpu.get_barrier_semaphore()
    for device in (after, before):
        pl.semaphore_signal(barrier, inc=1, device_id=device, device_id_type=MESH)
    for step in range(1, n_narrow):
        pl.semaphore_signal(
            barrier, inc=1, device_id=(g, lax.rem(n + step, n_narrow)), device_id_type=MESH
        )
    for step in range(1, n_wide):
        pl.semaphore_signal(
            barrier, inc=1, device_id=(lax.rem(g + step, n_wide), n), device_id_type=MESH
        )
    pl.semaphore_wait(barrier, n_narrow + n_wide)

    def send(source, low, high, at):
        copies = []
        for target, device, k in ((low, after, 2 * at), (high, before, 2 * at + 1)):
            copy = pltpu.make_async_remote_copy(
                src_ref=source,
                dst_ref=target,
                send_sem=halo_send.at[k],
                recv_sem=halo_recv.at[k],
                device_id=device,
                device_id_type=MESH,
            )
            copy.start()
            copies.append(copy)
        return copies

    halo = send(points, points_low, points_high, 0)
    halo += send(charges, charges_low, charges_high, 1)
    halo += send(leaf_skel, skel_low, skel_high, 2)

    load_basis.wait()

    def upward(i, total):
        first = charges[:, pl.ds(pl.multiple_of(i * 256, 256), 128)]
        second = charges[:, pl.ds(pl.multiple_of(i * 256 + 128, 128), 128)]
        weights = jnp.concatenate([twice(first), twice(second)], axis=0)
        product = dot(weights, beside(basis[i]), NT)
        values = jnp.where(
            lane((16, 128)) < 64,
            product[0:16] + product[16:32],
            product[32:48] + product[48:64],
        )
        at = pl.ds(pl.multiple_of(i * 128, 128), 128)
        leaf_charges[:, at] = values
        return total + dot(twice(values), beside(leaf_upward[:, at]), NT)

    total = lax.fori_loop(
        0, basis.shape[0], upward, jnp.zeros((32, 64), F32), unroll=4
    )
    own = total[:16] + total[16:]
    own = jnp.concatenate([own, jnp.zeros_like(own)], axis=1)
    node_mine[...] = own
    halo += send(leaf_charges, leaf_low, leaf_high, 3)

    def gather(count, mine, table, device_of, place, send_sems, recv_sems):
        def one(step):
            return pltpu.make_async_remote_copy(
                src_ref=mine,
                dst_ref=table.at[place],
                send_sem=send_sems.at[step],
                recv_sem=recv_sems.at[step],
                device_id=device_of(step),
                device_id_type=MESH,
            )

        copies = [one(step) for step in range(1, count)]
        for copy in copies:
            copy.start()
        table[place] = mine[...]
        for copy in copies:
            copy.wait()

    gather(
        n_narrow, node_mine, nodes, lambda step: (g, lax.rem(n + step, n_narrow)), n, node_send, node_recv
    )
    load_upward.wait()
    group = jnp.zeros((16, 64), F32)
    for i, pair in enumerate(in_pairs(nodes, n_narrow)):
        group = group + dot(pair, own_upward[:, 128 * i : 128 * (i + 1)], NT, HIGH)
    group_mine[...] = jnp.concatenate([group, jnp.zeros_like(group)], axis=1)
    gather(
        n_wide, group_mine, groups, lambda step: (lax.rem(g + step, n_wide), n), g, group_send, group_recv
    )
    nodes_out[...] = nodes[...]
    groups_out[...] = groups[...]
    for copy in halo:
        copy.wait()


def source_tile(ref, start, width):
    return [
        jnp.broadcast_to(ref[k : k + 1, pl.ds(start, width)], (8, width)) for k in range(6)
    ]


def source_values(rows):
    y0, y1, y2, m0, m1, m2 = rows
    at = row(y0.shape)
    square = y0 * y0 + y1 * y1 + y2 * y2 + SMOOTH
    flux = (y0 * m0 + y1 * m1 + y2 * m2) * (-COEFFICIENT)
    one, zero = jnp.ones_like(y0), jnp.zeros_like(y0)

    def pick(*terms):
        out = zero
        for k in reversed(range(len(terms))):
            out = jnp.where(at == k, terms[k], out)
        return out

    return (
        pick(-2.0 * y0, -2.0 * y1, -2.0 * y2, square, one),
        pick(COEFFICIENT * m0, COEFFICIENT * m1, COEFFICIENT * m2, flux),
    )


def source_parts(values):
    first, second, third = pieces(values)
    return jnp.concatenate([first, second, third, first, second, first], axis=0).astype(BF16)


def target_parts(rows):
    x0, x1, x2 = rows[:3]
    at = row(x0.shape)
    square = x0 * x0 + x1 * x1 + x2 * x2
    values = jnp.where(at == 0, x0, jnp.where(at == 1, x1, jnp.where(at == 2, x2, 0.0)))
    values = jnp.where(at == 3, 1.0, jnp.where(at == 4, square, values))
    first, second, third = pieces(values)
    fill = jnp.zeros((80, values.shape[1]), F32)
    stacked = jnp.concatenate([first, first, first, second, second, third, fill], axis=0)
    return stacked.T.astype(BF16)[:, :48]


def block(targets, sources):
    both = dot(targets, sources, NN)
    width = both.shape[1] // 2
    root = lax.rsqrt(both[:, :width])
    return beside((both[:, width:] * root) * (root * root))


def pair_kernel(target, source):
    offset = [target[:, k : k + 1] - source[k : k + 1] for k in range(3)]
    distance = offset[0] * offset[0] + offset[1] * offset[1] + offset[2] * offset[2] + SMOOTH
    flux = offset[0] * source[3:4] + offset[1] * source[4:5] + offset[2] * source[5:6]
    root = lax.rsqrt(distance)
    return (flux * root) * (root * root) * COEFFICIENT


def couplings(
    near_pairs,
    leaf_links,
    node_links,
    group_links,
    points_low,
    points_own,
    points_high,
    charges_low,
    charges_own,
    charges_high,
    skel_low,
    skel_own,
    skel_high,
    leaf_low,
    leaf_own,
    leaf_high,
    node_skel,
    group_skel,
    node_downward,
    nodes,
    groups,
    near,
    couple,
    fields,
    near_sources,
    near_weights,
    near_targets,
    far_sources,
    far_weights,
    far_targets,
):
    n_narrow = lax.axis_size("narrow")
    g, n = lax.axis_index("wide"), lax.axis_index("narrow")
    leaves = leaf_links.shape[0]
    first_leaf = (g * n_narrow + n) * leaves - leaves
    spare = 3 * leaves

    def half_of(skel, start, which):
        tile = source_tile(skel, pl.multiple_of(start, 128), 128)
        at = row((8, 128))
        values = jnp.where(at == 0, tile[0], jnp.where(at == 1, tile[1], tile[2]))
        values = jnp.where(which == 0, values, pltpu.roll(values, 64, 1))
        return values.T[:64]

    def marked(links, base, count):
        at = lane((1, 64 * count)) // 64
        hit = at < 0
        for k in range(links.shape[1]):
            hit = hit | (at == links[0, k] - base)
        return hit.astype(F32)

    def small(target, skel, values, mark):
        out = jnp.zeros((16, 64), F32)
        for i, value in enumerate(values):
            span = slice(128 * i, 128 * (i + 1))
            kernel = pair_kernel(target, skel[:, span]) * mark[:, span]
            out = out + dot(value, kernel, NT, HIGH)
        return out

    group_count = groups.shape[0]
    group_fields = small(
        half_of(group_skel, (g // 2) * 128, lax.rem(g, 2)),
        group_skel[...],
        in_pairs(groups, group_count),
        marked(group_links, 0, group_count),
    )
    own_span = pl.ds(pl.multiple_of(g * (64 * n_narrow), 128), 64 * n_narrow)
    node_fields = dot(group_fields, node_downward[...], NN, HIGH) + small(
        half_of(node_skel, g * (64 * n_narrow) + (n // 2) * 128, lax.rem(n, 2)),
        node_skel[:, own_span],
        in_pairs(nodes, n_narrow),
        marked(node_links, g * n_narrow, n_narrow),
    )
    fields[...] = node_fields

    near[...] = jnp.zeros_like(near)
    zero_rows = [jnp.zeros((8, 128), F32)] * 6
    for table in (near_sources, far_sources):
        parts = [source_parts(v) for v in source_values(zero_rows)]
        table[spare] = jnp.concatenate(parts, axis=1)
    for table in (near_weights, far_weights):
        table[spare] = jnp.zeros(table.shape[1:], BF16)

    for side, (points, charges) in enumerate(
        ((points_low, charges_low), (points_own, charges_own), (points_high, charges_high))
    ):

        def near_prepare(i, carry, side=side, points=points, charges=charges):
            start = pl.multiple_of(i * 128, 128)
            rows = source_tile(points, start, 128)
            parts = [source_parts(v) for v in source_values(rows)]
            near_sources[side * leaves + i] = jnp.concatenate(parts, axis=1)
            near_weights[side * leaves + i] = twice(charges[:, pl.ds(start, 128)])
            if side == 1:
                near_targets[i] = target_parts(rows)
            return carry

        lax.fori_loop(0, leaves, near_prepare, 0, unroll=4)

    def near_step(i, carry):
        parts = []
        for k in range(NEAR_STEP):
            code = near_pairs[0, i * NEAR_STEP + k]
            t, s = code // 1024, lax.rem(code, 1024)
            w = jnp.where(s >= 256, spare, s)
            s = jnp.where(s >= 256, spare, s)
            sums = dot(near_weights[w], block(near_targets[t], near_sources[s]), NT)
            parts.append((t, sums[:16] + sums[16:]))
        for t, part in parts:
            at = pl.ds(pl.multiple_of(t * 128, 128), 128)
            near[:, at] = near[:, at] + part
        return carry

    lax.fori_loop(0, NEAR_PAIRS // NEAR_STEP, near_step, 0)

    def both_halves(x):
        low = lane(x.shape) < 64
        turned = pltpu.roll(x, 64, 1)
        return jnp.where(low, x, turned), jnp.where(low, turned, x)

    for side, (points, charges) in enumerate(
        ((skel_low, leaf_low), (skel_own, leaf_own), (skel_high, leaf_high))
    ):

        def far_prepare(i, carry, side=side, points=points, charges=charges):
            start = pl.multiple_of(i * 128, 128)
            rows = source_tile(points, start, 128)
            split = [both_halves(v) for v in source_values(rows)]
            weights = both_halves(charges[:, pl.ds(start, 128)])
            for k in range(2):
                parts = [source_parts(v[k]) for v in split]
                far_sources[side * leaves + 2 * i + k] = jnp.concatenate(parts, axis=1)
                far_weights[side * leaves + 2 * i + k] = twice(weights[k])
            if side == 1:
                targets = target_parts(rows)
                far_targets[2 * i] = targets[:64]
                far_targets[2 * i + 1] = targets[64:]
            return carry

        lax.fori_loop(0, leaves // 2, far_prepare, 0, unroll=2)

    low_s = (lax.rem(lane((48, 256)), 128) < 64).astype(F32).astype(BF16)
    high_s = jnp.ones_like(low_s) - low_s
    low_w, high_w = low_s[:32], high_s[:32]

    def local(leaf, slot):
        entry = leaf_links[leaf, slot]
        return jnp.where(entry < 0, spare, entry - first_leaf)

    def far_step(i, carry):
        sums = []
        for k in range(2):
            leaf = 2 * i + k
            out = jnp.zeros((32, 64), F32)
            for slot in range(0, leaf_links.shape[1], 2):
                a, b = local(leaf, slot), local(leaf, slot + 1)
                sources = far_sources[a] * low_s + far_sources[b] * high_s
                weights = far_weights[a] * low_w + far_weights[b] * high_w
                out = out + dot(weights, block(far_targets[leaf], sources), NT)
            sums.append(out[:16] + out[16:])
        couple[:, pl.ds(pl.multiple_of(i * 128, 128), 128)] = jnp.concatenate(sums, axis=1)
        return carry

    lax.fori_loop(0, leaves // 2, far_step, 0)


def compact(near_list, first_leaf, leaves):
    flat = near_list.reshape(-1)
    count = flat.shape[0]
    used = flat >= 0
    ids = jnp.arange(count, dtype=jnp.int32)
    code = (ids // near_list.shape[1]) * 1024 + flat - first_leaf
    earlier = (ids[None, :] < ids[:, None]) & used[None, :]
    place = jnp.where(used, jnp.sum(earlier.astype(jnp.int32), axis=1), -1)
    slots = jnp.arange(NEAR_PAIRS, dtype=jnp.int32)
    hit = place[None, :] == slots[:, None]
    packed = jnp.sum(jnp.where(hit, code[None, :], 0), axis=1)
    total = jnp.sum(used.astype(jnp.int32))
    return jnp.where(slots < total, packed, 256)[None, :]


def on_device(
    points,
    charges,
    leaf_skel,
    node_skel,
    group_skel,
    source_basis,
    target_basis,
    leaf_upward,
    leaf_downward,
    node_upward,
    node_downward,
    near_list,
    leaf_links,
    node_links,
    group_links,
):
    n_wide, n_narrow = lax.axis_size("wide"), lax.axis_size("narrow")
    leaves, rank = source_basis.shape[0], source_basis.shape[1]
    first_leaf = (lax.axis_index("wide") * n_narrow + lax.axis_index("narrow")) * leaves - leaves
    vmem = pl.BlockSpec(memory_space=pltpu.VMEM)
    smem = pl.BlockSpec(memory_space=pltpu.SMEM)
    anywhere = pl.BlockSpec(memory_space=pl.ANY)

    def like(x):
        return jax.ShapeDtypeStruct(x.shape, F32)

    leaf_shape = jax.ShapeDtypeStruct((16, leaf_skel.shape[1]), F32)
    table = (16, 128)
    out = pl.pallas_call(
        exchange,
        out_shape=[
            like(points),
            like(points),
            like(charges),
            like(charges),
            like(leaf_skel),
            like(leaf_skel),
            leaf_shape,
            leaf_shape,
            leaf_shape,
            jax.ShapeDtypeStruct((n_narrow, *table), F32),
            jax.ShapeDtypeStruct((n_wide, *table), F32),
        ],
        in_specs=[anywhere, vmem, anywhere, anywhere, vmem, anywhere],
        out_specs=[anywhere] * 8 + [vmem] * 3,
        scratch_shapes=[
            pltpu.VMEM((leaves // 2, 2 * rank, source_basis.shape[2]), F32),
            pltpu.VMEM((64, 64 * n_narrow), F32),
            pltpu.VMEM((n_narrow, *table), F32),
            pltpu.VMEM((n_wide, *table), F32),
            pltpu.VMEM(table, F32),
            pltpu.VMEM(table, F32),
            pltpu.SemaphoreType.DMA((2,)),
            pltpu.SemaphoreType.DMA((8,)),
            pltpu.SemaphoreType.DMA((8,)),
            pltpu.SemaphoreType.DMA((n_narrow,)),
            pltpu.SemaphoreType.DMA((n_narrow,)),
            pltpu.SemaphoreType.DMA((n_wide,)),
            pltpu.SemaphoreType.DMA((n_wide,)),
        ],
        compiler_params=pltpu.CompilerParams(
            collective_id=0, has_side_effects=True, vmem_limit_bytes=VMEM_LIMIT
        ),
        name="exchange",
    )(
        points,
        charges,
        leaf_skel,
        source_basis.reshape(leaves // 2, 2 * rank, source_basis.shape[2]),
        leaf_upward,
        node_upward,
    )
    p_low, p_high, c_low, c_high, s_low, s_high, l_low, l_high, l_own, nodes, groups = out

    tables = 3 * leaves + 1
    near, couple, fields = pl.pallas_call(
        couplings,
        out_shape=[
            like(charges),
            leaf_shape,
            jax.ShapeDtypeStruct((16, rank), F32),
        ],
        in_specs=[smem] * 4 + [vmem] * 17,
        out_specs=[vmem] * 3,
        scratch_shapes=[
            pltpu.VMEM((tables, 48, 256), BF16),
            pltpu.VMEM((tables, 32, 256), BF16),
            pltpu.VMEM((leaves, 128, 48), BF16),
            pltpu.VMEM((tables, 48, 256), BF16),
            pltpu.VMEM((tables, 32, 256), BF16),
            pltpu.VMEM((leaves, 64, 48), BF16),
        ],
        compiler_params=pltpu.CompilerParams(vmem_limit_bytes=VMEM_LIMIT),
        name="couplings",
    )(
        compact(near_list, first_leaf, leaves),
        leaf_links,
        node_links,
        group_links,
        p_low,
        points,
        p_high,
        c_low,
        charges,
        c_high,
        s_low,
        leaf_skel,
        s_high,
        l_low,
        l_own,
        l_high,
        node_skel,
        group_skel,
        node_downward,
        nodes,
        groups,
    )
    leaf_fields = (jnp.dot(fields, leaf_downward, precision=HIGH) + couple).reshape(16, leaves, rank)
    far = jnp.einsum("qlr,lrp->qlp", leaf_fields, target_basis, precision=HIGH)
    return near + far.reshape(near.shape)


def solution(mesh):
    both = ("wide", "narrow")
    in_specs = (
        P(None, both),
        P(None, both),
        P(None, both),
        P(),
        P(),
        P(both, None, None),
        P(both, None, None),
        P(None, both),
        P(None, both),
        P(),
        P(None, both),
        P(both, None),
        P(both, None),
        P(both, None),
        P("wide", None),
    )
    return jax.shard_map(
        on_device, mesh=mesh, in_specs=in_specs, out_specs=P(None, both), check_vma=False
    )
```

time: 419 us -> 88.3 us (0.21)
  other arithmetic: 140 us -> 3.89 us
  matrix products: 117 us -> 3.72 us
  local copies, waits for them, and re-layouts: 101 us -> 2.46 us
  Pallas kernels: 0 us -> 77.7 us
  blocking collectives: 46.3 us -> 0 us
  starting transfers between devices: 10.4 us -> 0 us
    reduce_sum x18 -> x3, other arithmetic: 117 us -> 1.79 us  [the longest x1 1.47 us: compact(): total = jnp.sum(used.astype(jnp.int32))]
    dot_general x24 -> x2, matrix products: 117 us -> 3.72 us  [the longest x1 2.15 us: on_device(): far = jnp.einsum('qlr,lrp->qlp', leaf_fields, target_basis, precision=HIGH)]
    pallas_call x0 -> x2, Pallas kernels: none -> 77.7 us  [the longest x1 46.5 us: on_device(): pl.pallas_call(couplings, out_shape=[like(charges), leaf_shape, jax.Shape...]
    gather x68 -> x0, local copies, waits for them, and re-layouts: 65.5 us -> none  [the longest x8 18.1 us: far_block(): sources = skeleton_cube[:, picked]]
    all_gather x2 -> x0, blocking collectives: 46.3 us -> none  [the longest x1 29.1 us: on_device(): group_charges = lax.all_gather(own_group[None], 'wide', axis=0, tiled=True)]
    concatenate x20 -> x0, other arithmetic: 15.6 us -> none  [the longest x8 5.13 us: far_block(): leaf_cube[:3, leaf_ids][:, :, None, :]]
    dynamic_slice x19 -> x0, local copies, waits for them, and re-layouts: 10.9 us -> none  [the longest x16 9.89 us: on_device(): near_part = lax.map(near_block, near_starts)]
    ppermute x4 -> x0, starting transfers between devices: 10.4 us -> none  [the longest x2 7.71 us: with_halo(): lax.ppermute(lax.slice_in_dim(block, block.shape[dim] - width, None, axis...]
  transfers between devices with their start and end apart: 4 -> 0, of which waited for: 0 -> 0; matrix products, arithmetic and copies ran while one was open for 39% -> 0% of each run, Pallas kernels for 0% -> 0%
where the time goes in v1:
time: 88.3 us; the launch traced here: 87.8 us
  Pallas kernels  77.7 us (88%)
  other arithmetic  3.89 us (4%)
  matrix products  3.72 us (4%)
  local copies, waits for them, and re-layouts  2.46 us (3%)
    pallas_call x1, Pallas kernels, on_device(): pl.pallas_call(couplings, out_shape=[like(charges), leaf_shape, jax.Shape...  46.5 us
    pallas_call x1, Pallas kernels, on_device(): pl.pallas_call(exchange, out_shape=[like(points), like(points), like(char...  31.2 us
    unnamed x8, local copies, waits for them, and re-layouts  2.15 us
    dot_general x1, matrix products, on_device(): far = jnp.einsum('qlr,lrp->qlp', leaf_fields, target_basis, precision=HIGH)  2.15 us

profile of v1, /device:TPU:0, one launch (start us, length us, event | category | flops | bytes accessed | tf_op | source)
XLA Modules:
  0.0 87.8 jit_solution(606173144477996979)
XLA Ops:
  0.0 0.0 copy-start
  0.0 1.5 %convert_reduce_fusion.1 = s32[]{:T(128)} fusion(s32[64,8]{0,1:T(8,128)} %param.26), kind=kLoop, calls=%fused_computation.13 | loop fusion | flops 1535 | bytes 2052 | tf_op jit(solution)/shard_map/reduce_sum | solution.py:441
  1.5 1.4 %copy.24.leaf_links = s32[64,8]{1,0:T(8,128)} copy(s32[64,8]{0,1:T(8,128)} %param.27) | data formatting | bytes 4096 | tf_op args[12]
  2.8 0.8 copy.23
  3.6 0.1 reshape.57
  3.7 0.2 convert_reduce_fusion
  3.9 0.2 select_reduce_fusion
  4.1 1.2 %compare_select_fusion.near_pairs = s32[1,288]{1,0:T(1,128)} fusion(s32[288]{0:T(512)S(1)} %select_reduce_fusion, s32[]{:T(128)} %convert_reduce_fusion.1), kind=kLoop, calls=%fused_computation.9 | loop fusion | flops 576 | bytes 2308 | tf_op jit(solution)/shard_map/jit(_where)/select_n | solution.py:442
  5.3 31.2 %exchange.1 = (f32[6,8192]{1,0:T(8,128)}, f32[6,8192]{1,0:T(8,128)}, f32[16,8192]{1,0:T(8,128)}, f32[16,8192]{1,0:T(8,128)}, f32[6,4096]{1,0:T(8,128)}, /*index=...) custom-call(f32[6,8192]{1,0:T(8,128)} %points_own.1, ...), custom_call_target="tpu_custom_call" | custom-call | tf_op jit(solution)/shard_map/exchange/pallas_call | solution.py:474
  36.5 0.0 copy-start.1
  36.5 46.5 %couplings.1 = (f32[16,8192]{1,0:T(8,128)}, f32[16,4096]{1,0:T(8,128)}, f32[16,64]{1,0:T(8,128)}) custom-call(s32[1,288]{1,0:T(1,128)} %compare_select_fusion.near_pairs, s32[64,8]{1,0:T(8,128)} %copy.24.leaf_links, s32[1,4]{1,0:T(1,128)} %node_links.1, s32[1,8]{1,0:T(1,128)} %group_links.1, f32[6,8192]{1,0:T(8,128)} %get-tuple-element.19.points_low, ...), custom_call_target="tpu_custom_call" | custom-call | tf_op jit(solution)/shard_map/couplings/pallas_call | solution.py:521
  83.0 0.0 copy-done.1
  83.0 1.6 %convolution_add_fusion = f32[16,4096]{1,0:T(8,128)S(1)} fusion(f32[16,4096]{1,0:T(8,128)} %get-tuple-element.32, f32[16,64]{1,0:T(8,128)} %get-tuple-element.31, f32[64,4096]{1,0:T(8,128)S(1)} %copy-done.1), kind=kOutput, calls=%fused_computation | convolution fusion | flops 50397184 | bytes 1576960 | tf_op jit(solution)/shard_map/dot_general | solution.py:563
  84.6 0.0 copy-start.2
  84.6 0.2 reshape.59
  84.8 0.0 copy-done
  84.8 2.1 %convolution_bitcast_fusion = f32[64,2,8,128]{3,2,1,0:T(8,128)S(1)} fusion(f32[64,64,128]{2,1,0:T(8,128)S(1)} %copy-done, f32[16,64,64]{2,1,0:T(8,128)S(1)} %reshape.59), kind=kOutput, calls=%fused_computation.1 | convolution fusion | flops 100663296 | bytes 2883584 | tf_op jit(solution)/shard_map/qlr,lrp->qlp/dot_general | solution.py:564
  87.0 0.0 copy-done.2
  87.0 0.8 bitcast_add_fusion
  (2 shorter events, 0.0 us)
Async XLA Ops:
  0.0 84.8 %copy-start = (f32[64,64,128]{2,1,0:T(8,128)S(1)}, f32[64,64,128]{2,1,0:T(8,128)}, u32[]{:S(2)}) copy-start(f32[64,64,128]{2,1,0:T(8,128)} %param.21) | copy-start | bytes 6291460
  36.5 46.5 %copy-start.1 = (f32[64,4096]{1,0:T(8,128)S(1)}, f32[64,4096]{1,0:T(8,128)}, u32[]{:S(2)}) copy-start(f32[64,4096]{1,0:T(8,128)} %param.23) | copy-start | bytes 3145732
  84.6 2.4 %copy-start.2 = (f32[16,8192]{1,0:T(8,128)S(1)}, f32[16,8192]{1,0:T(8,128)}, u32[]{:S(2)}) copy-start(f32[16,8192]{1,0:T(8,128)} %get-tuple-element.30) | copy-start | bytes 1572868

commit v2 on v0

v2 whole, which is shorter than its diff:
```python
import math

import jax
import jax.numpy as jnp
from jax import lax
from jax.experimental import pallas as pl
from jax.experimental.pallas import tpu as pltpu
from jax.sharding import PartitionSpec as P

MESH = pl.DeviceIdType.MESH
HIGH = lax.Precision.HIGHEST
F32, BF16 = jnp.float32, jnp.bfloat16
SMOOTH = 0.25
COEFFICIENT = 1.0 / (4.0 * math.pi)
NT = (((1,), (1,)), ((), ()))
NN = (((1,), (0,)), ((), ()))
NEAR_REST = 288 - 64
NEAR_STEP = 32
FAR_STEP = 8
VMEM_LIMIT = 56 * 2**20


def dot(a, b, dims, precision=None):
    return lax.dot_general(a, b, dims, precision=precision, preferred_element_type=F32)


def halves(x):
    high = x.astype(BF16)
    return high, (x - high.astype(F32)).astype(BF16)


def twice(x):
    high, low = halves(x)
    stacked = jnp.concatenate([high, low], axis=0)
    return jnp.concatenate([stacked, stacked], axis=1)


def beside(x):
    high, low = halves(x)
    return jnp.concatenate([high, low], axis=1)


def pieces(x):
    first = x.astype(BF16).astype(F32)
    rest = x - first
    second = rest.astype(BF16).astype(F32)
    return first, second, rest - second


def lane(shape):
    return lax.broadcasted_iota(jnp.int32, shape, 1)


def row(shape):
    return lax.broadcasted_iota(jnp.int32, shape, 0)


def in_pairs(ref, count):
    return [
        ref[2 * i] + pltpu.roll(ref[2 * i + 1], 64, 1) for i in range(count // 2)
    ]


def source_tile(ref, start, width):
    return [
        jnp.broadcast_to(ref[k : k + 1, pl.ds(start, width)], (8, width)) for k in range(6)
    ]


def source_values(rows):
    y0, y1, y2, m0, m1, m2 = rows
    at = row(y0.shape)
    square = y0 * y0 + y1 * y1 + y2 * y2 + SMOOTH
    flux = (y0 * m0 + y1 * m1 + y2 * m2) * (-COEFFICIENT)
    one, zero = jnp.ones_like(y0), jnp.zeros_like(y0)

    def pick(*terms):
        out = zero
        for k in reversed(range(len(terms))):
            out = jnp.where(at == k, terms[k], out)
        return out

    return (
        pick(-2.0 * y0, -2.0 * y1, -2.0 * y2, square, one),
        pick(COEFFICIENT * m0, COEFFICIENT * m1, COEFFICIENT * m2, flux),
    )


def source_parts(values):
    first, second, third = pieces(values)
    return jnp.concatenate([first, second, third, first, second, first], axis=0).astype(BF16)


def target_parts(rows):
    x0, x1, x2 = rows[:3]
    at = row(x0.shape)
    square = x0 * x0 + x1 * x1 + x2 * x2
    values = jnp.where(at == 0, x0, jnp.where(at == 1, x1, jnp.where(at == 2, x2, 0.0)))
    values = jnp.where(at == 3, 1.0, jnp.where(at == 4, square, values))
    first, second, third = pieces(values)
    fill = jnp.zeros((80, values.shape[1]), F32)
    stacked = jnp.concatenate([first, first, first, second, second, third, fill], axis=0)
    return stacked.T.astype(BF16)[:, :48]


def kernel_block(targets, sources):
    both = dot(targets, sources, NN)
    width = both.shape[1] // 2
    root = lax.rsqrt(both[:, :width])
    return beside((both[:, width:] * root) * (root * root))


def pair_kernel(target, source):
    offset = [target[:, k : k + 1] - source[k : k + 1] for k in range(3)]
    distance = offset[0] * offset[0] + offset[1] * offset[1] + offset[2] * offset[2] + SMOOTH
    flux = offset[0] * source[3:4] + offset[1] * source[4:5] + offset[2] * source[5:6]
    root = lax.rsqrt(distance)
    return (flux * root) * (root * root) * COEFFICIENT


def fused(
    near_codes,
    near_places,
    far_codes,
    node_links,
    group_links,
    points,
    charges,
    leaf_skel,
    source_basis,
    leaf_upward,
    node_upward,
    node_skel,
    target_basis,
    leaf_downward,
    node_downward,
    group_skel,
    out,
    p_low,
    p_own,
    p_high,
    c_low,
    c_own,
    c_high,
    s_low,
    s_own,
    s_high,
    l_low,
    l_own,
    l_high,
    basis_up,
    basis_down,
    upward_own,
    downward_own,
    group_upward,
    nodes_skel,
    nodes,
    groups,
    node_mine,
    group_mine,
    near_sources,
    near_weights,
    near_targets,
    near_blocks,
    near_parts,
    far_sources,
    far_weights,
    far_targets,
    far_blocks,
    couple,
    load_sem,
    halo_send,
    halo_recv,
    node_send,
    node_recv,
    group_send,
    group_recv,
):
    n_wide, n_narrow = lax.axis_size("wide"), lax.axis_size("narrow")
    g, n = lax.axis_index("wide"), lax.axis_index("narrow")
    leaves = far_codes.shape[1]
    spare = 3 * leaves
    at_end = (n == n_narrow - 1).astype(jnp.int32)
    at_start = (n == 0).astype(jnp.int32)
    after = (lax.rem(g + at_end, n_wide), lax.rem(n + 1, n_narrow))
    before = (
        lax.rem(g - at_start + n_wide, n_wide),
        lax.rem(n - 1 + n_narrow, n_narrow),
    )
    group_span = pl.ds(pl.multiple_of(g * (64 * n_narrow), 128), 64 * n_narrow)

    loads = []
    for k, (source, target) in enumerate(
        (
            (charges, c_own),
            (source_basis, basis_up),
            (leaf_upward, upward_own),
            (points, p_own),
            (leaf_skel, s_own),
            (node_upward.at[:, group_span], group_upward),
            (node_skel.at[:, group_span], nodes_skel),
            (leaf_downward, downward_own),
            (target_basis, basis_down),
        )
    ):
        copy = pltpu.make_async_copy(source, target, load_sem.at[k])
        copy.start()
        loads.append(copy)

    barrier = pltpu.get_barrier_semaphore()
    for device in (after, before):
        pl.semaphore_signal(barrier, inc=1, device_id=device, device_id_type=MESH)
    for step in range(1, n_narrow):
        pl.semaphore_signal(
            barrier, inc=1, device_id=(g, lax.rem(n + step, n_narrow)), device_id_type=MESH
        )
    for step in range(1, n_wide):
        pl.semaphore_signal(
            barrier, inc=1, device_id=(lax.rem(g + step, n_wide), n), device_id_type=MESH
        )
    pl.semaphore_wait(barrier, n_narrow + n_wide)

    def send(source, low, high, at):
        copies = []
        for target, device, k in ((low, after, 2 * at), (high, before, 2 * at + 1)):
            copy = pltpu.make_async_remote_copy(
                src_ref=source,
                dst_ref=target,
                send_sem=halo_send.at[k],
                recv_sem=halo_recv.at[k],
                device_id=device,
                device_id_type=MESH,
            )
            copy.start()
            copies.append(copy)
        return copies

    near_halo = send(points, p_low, p_high, 0) + send(charges, c_low, c_high, 1)

    for copy in loads[:3]:
        copy.wait()

    def upward(i, total):
        first = c_own[:, pl.ds(pl.multiple_of(i * 256, 256), 128)]
        second = c_own[:, pl.ds(pl.multiple_of(i * 256 + 128, 128), 128)]
        weights = jnp.concatenate([twice(first), twice(second)], axis=0)
        product = dot(weights, beside(basis_up[i]), NT)
        values = jnp.where(
            lane((16, 128)) < 64,
            product[0:16] + product[16:32],
            product[32:48] + product[48:64],
        )
        at = pl.ds(pl.multiple_of(i * 128, 128), 128)
        l_own[:, at] = values
        return total + dot(twice(values), beside(upward_own[:, at]), NT)

    total = lax.fori_loop(0, leaves // 2, upward, jnp.zeros((32, 64), F32), unroll=8)
    own = total[:16] + total[16:]
    node_mine[...] = jnp.concatenate([own, jnp.zeros_like(own)], axis=1)

    def gather(count, mine, table, device_of, place, send_sems, recv_sems):
        copies = []
        for step in range(1, count):
            copy = pltpu.make_async_remote_copy(
                src_ref=mine,
                dst_ref=table.at[place],
                send_sem=send_sems.at[step],
                recv_sem=recv_sems.at[step],
                device_id=device_of(step),
                device_id_type=MESH,
            )
            copy.start()
            copies.append(copy)
        table[place] = mine[...]
        return copies

    node_copies = gather(
        n_narrow, node_mine, nodes, lambda step: (g, lax.rem(n + step, n_narrow)), n, node_send, node_recv
    )
    far_halo = send(leaf_skel, s_low, s_high, 2) + send(l_own, l_low, l_high, 3)

    zero_rows = [jnp.zeros((8, 128), F32)] * 6
    for table in (near_sources, far_sources):
        parts = [source_parts(v) for v in source_values(zero_rows)]
        table[spare] = jnp.concatenate(parts, axis=1)
    for table in (near_weights, far_weights):
        table[spare] = jnp.zeros(table.shape[1:], BF16)

    def prepare_near(side, points_ref, charges_ref):
        def body(i, carry):
            start = pl.multiple_of(i * 128, 128)
            rows = source_tile(points_ref, start, 128)
            parts = [source_parts(v) for v in source_values(rows)]
            near_sources[side * leaves + i] = jnp.concatenate(parts, axis=1)
            near_weights[side * leaves + i] = twice(charges_ref[:, pl.ds(start, 128)])
            if side == 1:
                near_targets[i] = target_parts(rows)
            return carry

        lax.fori_loop(0, leaves, body, 0, unroll=4)

    def both_halves(x):
        low = lane(x.shape) < 64
        turned = pltpu.roll(x, 64, 1)
        return jnp.where(low, x, turned), jnp.where(low, turned, x)

    def prepare_far(side, points_ref, charges_ref):
        def body(i, carry):
            start = pl.multiple_of(i * 128, 128)
            rows = source_tile(points_ref, start, 128)
            split = [both_halves(v) for v in source_values(rows)]
            weights = both_halves(charges_ref[:, pl.ds(start, 128)])
            for k in range(2):
                parts = [source_parts(v[k]) for v in split]
                far_sources[side * leaves + 2 * i + k] = jnp.concatenate(parts, axis=1)
                far_weights[side * leaves + 2 * i + k] = twice(weights[k])
            if side == 1:
                targets = target_parts(rows)
                far_targets[2 * i] = targets[:64]
                far_targets[2 * i + 1] = targets[64:]
            return carry

        lax.fori_loop(0, leaves // 2, body, 0, unroll=4)

    def stream(count, first, second):
        first(0)

        def body(i, carry):
            second(i - 1)
            first(i)
            return carry

        lax.fori_loop(1, count, body, 0)
        second(count - 1)

    loads[3].wait()
    prepare_near(1, p_own, c_own)

    def self_first(i):
        for k in range(NEAR_STEP):
            leaf = i * NEAR_STEP + k
            near_blocks[k] = kernel_block(near_targets[leaf], near_sources[leaves + leaf])

    def self_second(i):
        for k in range(NEAR_STEP):
            leaf = i * NEAR_STEP + k
            sums = dot(near_weights[leaves + leaf], near_blocks[k], NT)
            out[:, pl.ds(pl.multiple_of(leaf * 128, 128), 128)] = sums[:16] + sums[16:]

    stream(leaves // NEAR_STEP, self_first, self_second)

    loads[4].wait()
    prepare_far(1, s_own, l_own)

    for copy in node_copies:
        copy.wait()
    loads[5].wait()
    group = jnp.zeros((16, 64), F32)
    for i, pair in enumerate(in_pairs(nodes, n_narrow)):
        group = group + dot(pair, group_upward[:, 128 * i : 128 * (i + 1)], NT, HIGH)
    group_mine[...] = jnp.concatenate([group, jnp.zeros_like(group)], axis=1)
    group_copies = gather(
        n_wide, group_mine, groups, lambda step: (lax.rem(g + step, n_wide), n), g, group_send, group_recv
    )

    for copy in near_halo:
        copy.wait()
    prepare_near(0, p_low, c_low)
    prepare_near(2, p_high, c_high)

    def near_code(i, k):
        code = near_codes[0, i * NEAR_STEP + k]
        return code // 1024, lax.rem(code, 1024)

    def near_first(i):
        for k in range(NEAR_STEP):
            t, s = near_code(i, k)
            near_blocks[k] = kernel_block(near_targets[t], near_sources[s])

    def near_second(i):
        for k in range(NEAR_STEP):
            _, s = near_code(i, k)
            sums = dot(near_weights[s], near_blocks[k], NT)
            near_parts[i * NEAR_STEP + k] = sums[:16] + sums[16:]

    stream(NEAR_REST // NEAR_STEP, near_first, near_second)
    near_parts[NEAR_REST] = jnp.zeros((16, 128), F32)

    for copy in far_halo:
        copy.wait()
    prepare_far(0, s_low, l_low)
    prepare_far(2, s_high, l_high)

    low_s = (lax.rem(lane((48, 256)), 128) < 64).astype(F32).astype(BF16)
    high_s = jnp.ones_like(low_s) - low_s
    low_w, high_w = low_s[:32], high_s[:32]
    far_slots = far_codes.shape[0]

    def far_picks(i):
        for k in range(FAR_STEP):
            for slot in range(0, far_slots, 2):
                leaf = FAR_STEP * i + k
                yield k, slot // 2, leaf, far_codes[slot, leaf], far_codes[slot + 1, leaf]

    def far_first(i):
        for k, j, leaf, a, b in far_picks(i):
            sources = far_sources[a] * low_s + far_sources[b] * high_s
            far_blocks[k * (far_slots // 2) + j] = kernel_block(far_targets[leaf], sources)

    def far_second(i):
        sums = [jnp.zeros((32, 64), F32)] * FAR_STEP
        for k, j, _, a, b in far_picks(i):
            weights = far_weights[a] * low_w + far_weights[b] * high_w
            sums[k] = sums[k] + dot(weights, far_blocks[k * (far_slots // 2) + j], NT)
        sums = [x[:16] + x[16:] for x in sums]
        for k in range(0, FAR_STEP, 2):
            at = pl.ds(pl.multiple_of((FAR_STEP * i + k) * 64, 128), 128)
            couple[:, at] = jnp.concatenate(sums[k : k + 2], axis=1)

    stream(leaves // FAR_STEP, far_first, far_second)

    for copy in group_copies:
        copy.wait()
    loads[6].wait()

    def half_of(skel, start, which):
        tile = source_tile(skel, pl.multiple_of(start, 128), 128)
        at = row((8, 128))
        values = jnp.where(at == 0, tile[0], jnp.where(at == 1, tile[1], tile[2]))
        values = jnp.where(which == 0, values, pltpu.roll(values, 64, 1))
        return values.T[:64]

    def marked(links, base, count):
        at = lane((1, 64 * count)) // 64
        hit = at < 0
        for k in range(links.shape[1]):
            hit = hit | (at == links[0, k] - base)
        return hit.astype(F32)

    def small(target, skel, values, mark):
        sums = jnp.zeros((16, 64), F32)
        for i, value in enumerate(values):
            span = slice(128 * i, 128 * (i + 1))
            kernel = pair_kernel(target, skel[:, span]) * mark[:, span]
            sums = sums + dot(value, kernel, NT, HIGH)
        return sums

    group_fields = small(
        half_of(group_skel, (g // 2) * 128, lax.rem(g, 2)),
        group_skel[...],
        in_pairs(groups, n_wide),
        marked(group_links, 0, n_wide),
    )
    node_fields = dot(group_fields, node_downward[...], NN, HIGH) + small(
        half_of(nodes_skel, (n // 2) * 128, lax.rem(n, 2)),
        nodes_skel[...],
        in_pairs(nodes, n_narrow),
        marked(node_links, g * n_narrow, n_narrow),
    )
    field_halves = jnp.concatenate(halves(node_fields), axis=0)

    loads[7].wait()
    loads[8].wait()

    def downward(i, carry):
        at = pl.ds(pl.multiple_of(i * 128, 128), 128)
        product = dot(field_halves, beside(downward_own[:, at]), NN)
        fields = product[:16, :128] + product[16:, :128] + product[:16, 128:] + couple[:, at]
        low = lane((16, 128)) < 64
        lefts = [jnp.where(low, fields, 0.0), jnp.where(low, 0.0, fields)]
        left = jnp.concatenate([h for x in lefts for h in halves(x)], axis=0)
        product = dot(left, beside(basis_down[i]), NN)
        for k in range(2):
            leaf = 2 * i + k
            rows = product[32 * k : 32 * (k + 1)]
            value = rows[:16, :128] + rows[16:, :128] + rows[:16, 128:]
            for slot in range(near_places.shape[0]):
                value = value + near_parts[near_places[slot, leaf]]
            span = pl.ds(pl.multiple_of(leaf * 128, 128), 128)
            out[:, span] = out[:, span] + value
        return carry

    lax.fori_loop(0, leaves // 2, downward, 0, unroll=4)


def compact(near_list, first_leaf, leaves):
    rest = near_list.T[1:]
    flat = rest.reshape(-1)
    used = flat >= 0
    ids = jnp.arange(flat.shape[0], dtype=jnp.int32)
    code = lax.rem(ids, leaves) * 1024 + flat - first_leaf
    earlier = (ids[None, :] < ids[:, None]) & used[None, :]
    place = jnp.where(used, jnp.sum(earlier.astype(jnp.int32), axis=1), NEAR_REST)
    slots = jnp.arange(NEAR_REST, dtype=jnp.int32)
    hit = place[None, :] == slots[:, None]
    packed = jnp.sum(jnp.where(hit, code[None, :] + 1, 0), axis=1)
    codes = jnp.where(packed > 0, packed - 1, 3 * leaves)
    return codes[None, :], place.reshape(rest.shape)


def on_device(
    points,
    charges,
    leaf_skel,
    node_skel,
    group_skel,
    source_basis,
    target_basis,
    leaf_upward,
    leaf_downward,
    node_upward,
    node_downward,
    near_list,
    leaf_links,
    node_links,
    group_links,
):
    n_wide, n_narrow = lax.axis_size("wide"), lax.axis_size("narrow")
    leaves, rank, size = source_basis.shape
    first_leaf = (lax.axis_index("wide") * n_narrow + lax.axis_index("narrow")) * leaves - leaves
    vmem = pl.BlockSpec(memory_space=pltpu.VMEM)
    smem = pl.BlockSpec(memory_space=pltpu.SMEM)
    anywhere = pl.BlockSpec(memory_space=pl.ANY)
    tables = 3 * leaves + 1
    table = (16, 128)
    paired = (leaves // 2, 2 * rank, size)
    codes, places = compact(near_list, first_leaf, leaves)

    def f32(*shape):
        return pltpu.VMEM(shape, F32)

    def bf16(*shape):
        return pltpu.VMEM(shape, BF16)

    def sems(count):
        return pltpu.SemaphoreType.DMA((count,))

    return pl.pallas_call(
        fused,
        out_shape=jax.ShapeDtypeStruct(charges.shape, F32),
        in_specs=[smem] * 5 + [anywhere] * 9 + [vmem] * 2,
        out_specs=vmem,
        scratch_shapes=[
            *[f32(*points.shape)] * 3,
            *[f32(*charges.shape)] * 3,
            *[f32(*leaf_skel.shape)] * 3,
            *[f32(16, leaf_skel.shape[1])] * 3,
            f32(*paired),
            f32(*paired),
            f32(*leaf_upward.shape),
            f32(*leaf_downward.shape),
            f32(64, 64 * n_narrow),
            f32(6, 64 * n_narrow),
            f32(n_narrow, *table),
            f32(n_wide, *table),
            f32(*table),
            f32(*table),
            bf16(tables, 48, 256),
            bf16(tables, 32, 256),
            bf16(leaves, 128, 48),
            bf16(NEAR_STEP, 128, 256),
            f32(NEAR_REST + 1, *table),
            bf16(tables, 48, 256),
            bf16(tables, 32, 256),
            bf16(leaves, 64, 48),
            bf16(4 * FAR_STEP, 64, 256),
            f32(16, leaf_skel.shape[1]),
            sems(9),
            sems(8),
            sems(8),
            sems(n_narrow),
            sems(n_narrow),
            sems(n_wide),
            sems(n_wide),
        ],
        compiler_params=pltpu.CompilerParams(
            collective_id=0, has_side_effects=True, vmem_limit_bytes=VMEM_LIMIT
        ),
        name="fused",
    )(
        codes,
        places,
        jnp.where(leaf_links < 0, 3 * leaves, leaf_links - first_leaf).T,
        node_links,
        group_links,
        points,
        charges,
        leaf_skel,
        source_basis.reshape(paired),
        leaf_upward,
        node_upward,
        node_skel,
        target_basis.reshape(paired),
        leaf_downward,
        node_downward,
        group_skel,
    )


def solution(mesh):
    both = ("wide", "narrow")
    in_specs = (
        P(None, both),
        P(None, both),
        P(None, both),
        P(),
        P(),
        P(both, None, None),
        P(both, None, None),
        P(None, both),
        P(None, both),
        P(),
        P(None, both),
        P(both, None),
        P(both, None),
        P(both, None),
        P("wide", None),
    )
    return jax.shard_map(
        on_device, mesh=mesh, in_specs=in_specs, out_specs=P(None, both), check_vma=False
    )
```

time: 419 us -> 54.1 us (0.13)
  the two profiles are of different devices: /device:TPU:0 before, /device:TPU:1 now
where the time goes in v2:
time: 54.1 us; the launch traced here: 53.8 us
  Pallas kernels  47.6 us (88%)
  other arithmetic  3.42 us (6%)
  local copies, waits for them, and re-layouts  2.71 us (5%)
    pallas_call x1, Pallas kernels, on_device(): pl.pallas_call(fused, out_shape=jax.ShapeDtypeStruct(charges.shape, F32),...  47.6 us
    unnamed x1, local copies, waits for them, and re-layouts  1.87 us
    select_n x1, other arithmetic, compact(): jnp.where(used, jnp.sum(earlier.astype(jnp.int32), axis=1), NEAR_REST)  1.28 us
    transpose x1, other arithmetic, on_device(): jnp.where(leaf_links < 0, 3 * leaves, leaf_links - first_leaf)  1.28 us

profile of v2, /device:TPU:1, one launch (start us, length us, event | category | flops | bytes accessed | tf_op | source)
XLA Modules:
  0.0 53.8 jit_solution(2124329078668557586)
XLA Ops:
  0.0 0.7 %slice.3 = s32[7,64]{1,0:T(8,128)S(1)} slice(s32[8,64]{1,0:T(8,128)} %bitcast.8), slice={[1:8], [0:64]} | slice | bytes 3584 | tf_op jit(solution)/shard_map/slice | solution.py:487
  0.7 0.1 reshape.54
  0.8 0.2 convert_reduce_fusion
  0.9 0.1 select_reduce_fusion
  1.1 0.6 %compare_select_fusion.1 = s32[224]{0:T(256)} fusion(s32[224]{0:T(256)S(1)} %select_reduce_fusion), kind=kLoop, calls=%fused_computation.8 | loop fusion | flops 672 | bytes 1792 | tf_op jit(solution)/shard_map/jit(_where)/select_n | solution.py:497
  1.6 0.1 reduce_sum.22
  1.7 1.3 %compare_select_fusion.near_places = s32[7,64]{1,0:T(8,128)} fusion(s32[7,64]{1,0:T(8,128)S(1)} %reduce_sum.22, s32[8,64]{1,0:T(8,128)} %bitcast.9), kind=kLoop, calls=%fused_computation.6 | loop fusion | flops 896 | bytes 5376 | tf_op jit(solution)/shard_map/jit(_where)/select_n | solution.py:493
  3.0 1.3 %select_bitcast_fusion.far_codes = s32[8,64]{1,0:T(8,128)} fusion(s32[64,8]{0,1:T(8,128)} %param.27, s32[]{:T(128)S(6)} %sub.23), kind=kLoop, calls=%fused_computation.5 | loop fusion | flops 1536 | bytes 4100 | tf_op jit(solution)/shard_map/transpose | solution.py:583
  4.3 47.6 %fused.1 = f32[16,8192]{1,0:T(8,128)} custom-call(s32[1,224]{1,0:T(1,128)} %bitcast.10, s32[7,64]{1,0:T(8,128)} %compare_select_fusion.near_places, s32[8,64]{1,0:T(8,128)} %select_bitcast_fusion.far_codes, s32[1,4]{1,0:T(1,128)} %node_links.1, s32[1,8]{1,0:T(1,128)} %group_links.1, f32[6,8192]{1,0:T(8,128)} %points.1, f32[16,8192]{1,0:T(8,128)} %charges.1, ...), custom_call_target="tpu_custom_call" | custom-call | tf_op jit(solution)/shard_map/fused/pallas_call | solution.py:538
  51.9 1.9 %copy.17 = f32[16,8192]{1,0:T(8,128)} copy(f32[16,8192]{1,0:T(8,128)} %fused.1) | data formatting | bytes 1048576
  (2 shorter events, 0.0 us)

commit v3 on v2

--- a/solution.py
+++ b/solution.py
@@ -118,10 +118,42 @@
     return (flux * root) * (root * root) * COEFFICIENT
 
 
+def lists(near, links, first_leaf):
+    slots, leaves = near.shape
+    fill = jnp.full((slots, 128 - leaves), -1, jnp.int32)
+    near = jnp.concatenate([near, fill], axis=1)
+    links = jnp.concatenate([links, fill], axis=1)
+    spare = 3 * leaves
+    far = jnp.where(links < 0, spare, jnp.clip(links - first_leaf, 0, spare - 1))
+    across, down = lane(near.shape), row(near.shape)
+    used = (near >= 0) & (down > 0)
+    count = used.astype(jnp.int32)
+    along = count
+    step = 1
+    while step < leaves:
+        along = along + jnp.where(across >= step, pltpu.roll(along, step, 1), 0)
+        step *= 2
+    totals = jnp.broadcast_to(along[:, leaves - 1 : leaves], along.shape)
+    above = totals
+    step = 1
+    while step < slots:
+        above = above + jnp.where(down >= step, pltpu.roll(above, step, 0), 0)
+        step *= 2
+    place = along - count + above - totals
+    place = jnp.where(used, jnp.minimum(place, NEAR_REST), NEAR_REST)
+    code = across * 1024 + jnp.clip(near - first_leaf, 0, spare - 1) + 1
+    places, codes = place.T[:leaves], code.T[:leaves]
+    at = lane((leaves, 256))
+    hits = jnp.zeros((leaves, 256), jnp.int32)
+    for slot in range(1, slots):
+        hits = hits + jnp.where(places[:, slot : slot + 1] == at, codes[:, slot : slot + 1], 0)
+    packed = jnp.sum(hits, axis=0, keepdims=True)
+    return jnp.where((packed > 0) & (lane((1, 256)) < NEAR_REST), packed - 1, spare), place, far
+
+
 def fused(
-    near_codes,
-    near_places,
-    far_codes,
+    near_list,
+    leaf_links,
     node_links,
     group_links,
     points,
@@ -135,7 +167,8 @@
     leaf_downward,
     node_downward,
     group_skel,
-    out,
+    near_out,
+    far_out,
     p_low,
     p_own,
     p_high,
@@ -168,7 +201,14 @@
     far_targets,
     far_blocks,
     couple,
+    near_codes_v,
+    near_places_v,
+    far_codes_v,
+    near_codes,
+    near_places,
+    far_codes,
     load_sem,
+    list_sem,
     halo_send,
     halo_recv,
     node_send,
@@ -178,8 +218,9 @@
 ):
     n_wide, n_narrow = lax.axis_size("wide"), lax.axis_size("narrow")
     g, n = lax.axis_index("wide"), lax.axis_index("narrow")
-    leaves = far_codes.shape[1]
+    leaves = leaf_links.shape[1]
     spare = 3 * leaves
+    first_leaf = (g * n_narrow + n) * leaves - leaves
     at_end = (n == n_narrow - 1).astype(jnp.int32)
     at_start = (n == 0).astype(jnp.int32)
     after = (lax.rem(g + at_end, n_wide), lax.rem(n + 1, n_narrow))
@@ -237,6 +278,16 @@
 
     near_halo = send(points, p_low, p_high, 0) + send(charges, c_low, c_high, 1)
 
+    codes, places, far = lists(near_list[...], leaf_links[...], first_leaf)
+    near_codes_v[...], near_places_v[...], far_codes_v[...] = codes, places, far
+    list_copies = []
+    for k, (source, target) in enumerate(
+        ((near_codes_v, near_codes), (near_places_v, near_places), (far_codes_v, far_codes))
+    ):
+        copy = pltpu.make_async_copy(source, target, list_sem.at[k])
+        copy.start()
+        list_copies.append(copy)
+
     for copy in loads[:3]:
         copy.wait()
 
@@ -345,7 +396,7 @@
         for k in range(NEAR_STEP):
             leaf = i * NEAR_STEP + k
             sums = dot(near_weights[leaves + leaf], near_blocks[k], NT)
-            out[:, pl.ds(pl.multiple_of(leaf * 128, 128), 128)] = sums[:16] + sums[16:]
+            near_out[:, pl.ds(pl.multiple_of(leaf * 128, 128), 128)] = sums[:16] + sums[16:]
 
     stream(leaves // NEAR_STEP, self_first, self_second)
 
@@ -355,14 +406,17 @@
     for copy in node_copies:
         copy.wait()
     loads[5].wait()
-    group = jnp.zeros((16, 64), F32)
-    for i, pair in enumerate(in_pairs(nodes, n_narrow)):
-        group = group + dot(pair, group_upward[:, 128 * i : 128 * (i + 1)], NT, HIGH)
+    group = dot(
+        twice(jnp.concatenate(in_pairs(nodes, n_narrow), axis=1)), beside(group_upward[...]), NT
+    )
+    group = group[:16] + group[16:]
     group_mine[...] = jnp.concatenate([group, jnp.zeros_like(group)], axis=1)
     group_copies = gather(
         n_wide, group_mine, groups, lambda step: (lax.rem(g + step, n_wide), n), g, group_send, group_recv
     )
 
+    for copy in list_copies:
+        copy.wait()
     for copy in near_halo:
         copy.wait()
     prepare_near(0, p_low, c_low)
@@ -394,7 +448,7 @@
     low_s = (lax.rem(lane((48, 256)), 128) < 64).astype(F32).astype(BF16)
     high_s = jnp.ones_like(low_s) - low_s
     low_w, high_w = low_s[:32], high_s[:32]
-    far_slots = far_codes.shape[0]
+    far_slots = leaf_links.shape[0]
 
     def far_picks(i):
         for k in range(FAR_STEP):
@@ -438,12 +492,9 @@
         return hit.astype(F32)
 
     def small(target, skel, values, mark):
-        sums = jnp.zeros((16, 64), F32)
-        for i, value in enumerate(values):
-            span = slice(128 * i, 128 * (i + 1))
-            kernel = pair_kernel(target, skel[:, span]) * mark[:, span]
-            sums = sums + dot(value, kernel, NT, HIGH)
-        return sums
+        kernel = pair_kernel(target, skel) * mark
+        sums = dot(twice(jnp.concatenate(values, axis=1)), beside(kernel), NT)
+        return sums[:16] + sums[16:]
 
     group_fields = small(
         half_of(group_skel, (g // 2) * 128, lax.rem(g, 2)),
@@ -474,28 +525,13 @@
             leaf = 2 * i + k
             rows = product[32 * k : 32 * (k + 1)]
             value = rows[:16, :128] + rows[16:, :128] + rows[:16, 128:]
-            for slot in range(near_places.shape[0]):
+            for slot in range(1, near_list.shape[0]):
                 value = value + near_parts[near_places[slot, leaf]]
             span = pl.ds(pl.multiple_of(leaf * 128, 128), 128)
-            out[:, span] = out[:, span] + value
+            far_out[:, span] = value
         return carry
 
     lax.fori_loop(0, leaves // 2, downward, 0, unroll=4)
-
-
-def compact(near_list, first_leaf, leaves):
-    rest = near_list.T[1:]
-    flat = rest.reshape(-1)
-    used = flat >= 0
-    ids = jnp.arange(flat.shape[0], dtype=jnp.int32)
-    code = lax.rem(ids, leaves) * 1024 + flat - first_leaf
-    earlier = (ids[None, :] < ids[:, None]) & used[None, :]
-    place = jnp.where(used, jnp.sum(earlier.astype(jnp.int32), axis=1), NEAR_REST)
-    slots = jnp.arange(NEAR_REST, dtype=jnp.int32)
-    hit = place[None, :] == slots[:, None]
-    packed = jnp.sum(jnp.where(hit, code[None, :] + 1, 0), axis=1)
-    codes = jnp.where(packed > 0, packed - 1, 3 * leaves)
-    return codes[None, :], place.reshape(rest.shape)
 
 
 def on_device(
@@ -517,14 +553,12 @@
 ):
     n_wide, n_narrow = lax.axis_size("wide"), lax.axis_size("narrow")
     leaves, rank, size = source_basis.shape
-    first_leaf = (lax.axis_index("wide") * n_narrow + lax.axis_index("narrow")) * leaves - leaves
     vmem = pl.BlockSpec(memory_space=pltpu.VMEM)
     smem = pl.BlockSpec(memory_space=pltpu.SMEM)
     anywhere = pl.BlockSpec(memory_space=pl.ANY)
     tables = 3 * leaves + 1
     table = (16, 128)
     paired = (leaves // 2, 2 * rank, size)
-    codes, places = compact(near_list, first_leaf, leaves)
 
     def f32(*shape):
         return pltpu.VMEM(shape, F32)
@@ -535,11 +569,11 @@
     def sems(count):
         return pltpu.SemaphoreType.DMA((count,))
 
-    return pl.pallas_call(
+    near, far = pl.pallas_call(
         fused,
-        out_shape=jax.ShapeDtypeStruct(charges.shape, F32),
-        in_specs=[smem] * 5 + [anywhere] * 9 + [vmem] * 2,
-        out_specs=vmem,
+        out_shape=[jax.ShapeDtypeStruct(charges.shape, F32)] * 2,
+        in_specs=[vmem] * 2 + [smem] * 2 + [anywhere] * 9 + [vmem] * 2,
+        out_specs=[vmem] * 2,
         scratch_shapes=[
             *[f32(*points.shape)] * 3,
             *[f32(*charges.shape)] * 3,
@@ -565,7 +599,14 @@
             bf16(leaves, 64, 48),
             bf16(4 * FAR_STEP, 64, 256),
             f32(16, leaf_skel.shape[1]),
+            pltpu.VMEM((1, 256), jnp.int32),
+            pltpu.VMEM((8, 128), jnp.int32),
+            pltpu.VMEM((8, 128), jnp.int32),
+            pltpu.SMEM((1, 256), jnp.int32),
+            pltpu.SMEM((8, 128), jnp.int32),
+            pltpu.SMEM((8, 128), jnp.int32),
             sems(9),
+            sems(3),
             sems(8),
             sems(8),
             sems(n_narrow),
@@ -578,9 +619,8 @@
         ),
         name="fused",
     )(
-        codes,
-        places,
-        jnp.where(leaf_links < 0, 3 * leaves, leaf_links - first_leaf).T,
+        near_list.T,
+        leaf_links.T,
         node_links,
         group_links,
         points,
@@ -595,6 +635,7 @@
         node_downward,
         group_skel,
     )
+    return near + far
 
 
 def solution(mesh):

time: 54.1 us -> 48.8 us (0.902)
  the two profiles are of different devices: /device:TPU:1 before, /device:TPU:0 now
where the time goes in v3:
time: 48.8 us; the launch traced here: 47.9 us
  Pallas kernels  45.8 us (94%)
  other arithmetic  2.05 us (4%)
    pallas_call x1, Pallas kernels, on_device(): pl.pallas_call(fused, out_shape=[jax.ShapeDtypeStruct(charges.shape, F32)...  45.8 us
    add x1, other arithmetic, on_device(): return near + far  2.05 us

profile of v3, /device:TPU:0, one launch (start us, length us, event | category | flops | bytes accessed | tf_op | source)
XLA Modules:
  0.0 47.9 jit_solution(15709840698213492484)
XLA Ops:
  0.0 45.8 %fused.1 = (f32[16,8192]{1,0:T(8,128)}, f32[16,8192]{1,0:T(8,128)}) custom-call(s32[8,64]{1,0:T(8,128)} %bitcast.6, s32[8,64]{1,0:T(8,128)} %bitcast.7, s32[1,4]{1,0:T(1,128)} %node_links.1, s32[1,8]{1,0:T(1,128)} %group_links.1, f32[6,8192]{1,0:T(8,128)} %points.1, f32[16,8192]{1,0:T(8,128)} %charges.1, f32[6,4096]{1,0:T(8,128)} %leaf_skel.1, ...), custom_call_target="tpu_custom_call" | custom-call | tf_op jit(solution)/shard_map/fused/pallas_call | solution.py:572
  45.9 2.0 %add.3 = f32[16,8192]{1,0:T(8,128)} add(f32[16,8192]{1,0:T(8,128)} %get-tuple-element.7, f32[16,8192]{1,0:T(8,128)} %get-tuple-element.8) | non-fusion elementwise | flops 131072 | bytes 1572864 | tf_op jit(solution)/shard_map/add | solution.py:638

commit v4 on v3

--- a/solution.py
+++ b/solution.py
@@ -17,6 +17,7 @@
 NEAR_REST = 288 - 64
 NEAR_STEP = 32
 FAR_STEP = 8
+FINISH_STEPS = 4
 VMEM_LIMIT = 56 * 2**20
 
 
@@ -163,12 +164,11 @@
     leaf_upward,
     node_upward,
     node_skel,
-    target_basis,
-    leaf_downward,
     node_downward,
     group_skel,
-    near_out,
-    far_out,
+    near,
+    couple,
+    fields,
     p_low,
     p_own,
     p_high,
@@ -182,9 +182,7 @@
     l_own,
     l_high,
     basis_up,
-    basis_down,
     upward_own,
-    downward_own,
     group_upward,
     nodes_skel,
     nodes,
@@ -200,7 +198,6 @@
     far_weights,
     far_targets,
     far_blocks,
-    couple,
     near_codes_v,
     near_places_v,
     far_codes_v,
@@ -240,8 +237,6 @@
             (leaf_skel, s_own),
             (node_upward.at[:, group_span], group_upward),
             (node_skel.at[:, group_span], nodes_skel),
-            (leaf_downward, downward_own),
-            (target_basis, basis_down),
         )
     ):
         copy = pltpu.make_async_copy(source, target, load_sem.at[k])
@@ -276,7 +271,8 @@
             copies.append(copy)
         return copies
 
-    near_halo = send(points, p_low, p_high, 0) + send(charges, c_low, c_high, 1)
+    near_halo = send(points, p_low, p_high, 0)
+    far_halo = send(leaf_skel, s_low, s_high, 2)
 
     codes, places, far = lists(near_list[...], leaf_links[...], first_leaf)
     near_codes_v[...], near_places_v[...], far_codes_v[...] = codes, places, far
@@ -328,7 +324,8 @@
     node_copies = gather(
         n_narrow, node_mine, nodes, lambda step: (g, lax.rem(n + step, n_narrow)), n, node_send, node_recv
     )
-    far_halo = send(leaf_skel, s_low, s_high, 2) + send(l_own, l_low, l_high, 3)
+    far_halo += send(l_own, l_low, l_high, 3)
+    near_halo += send(charges, c_low, c_high, 1)
 
     zero_rows = [jnp.zeros((8, 128), F32)] * 6
     for table in (near_sources, far_sources):
@@ -396,7 +393,7 @@
         for k in range(NEAR_STEP):
             leaf = i * NEAR_STEP + k
             sums = dot(near_weights[leaves + leaf], near_blocks[k], NT)
-            near_out[:, pl.ds(pl.multiple_of(leaf * 128, 128), 128)] = sums[:16] + sums[16:]
+            near[:, pl.ds(pl.multiple_of(leaf * 128, 128), 128)] = sums[:16] + sums[16:]
 
     stream(leaves // NEAR_STEP, self_first, self_second)
 
@@ -417,29 +414,6 @@
 
     for copy in list_copies:
         copy.wait()
-    for copy in near_halo:
-        copy.wait()
-    prepare_near(0, p_low, c_low)
-    prepare_near(2, p_high, c_high)
-
-    def near_code(i, k):
-        code = near_codes[0, i * NEAR_STEP + k]
-        return code // 1024, lax.rem(code, 1024)
-
-    def near_first(i):
-        for k in range(NEAR_STEP):
-            t, s = near_code(i, k)
-            near_blocks[k] = kernel_block(near_targets[t], near_sources[s])
-
-    def near_second(i):
-        for k in range(NEAR_STEP):
-            _, s = near_code(i, k)
-            sums = dot(near_weights[s], near_blocks[k], NT)
-            near_parts[i * NEAR_STEP + k] = sums[:16] + sums[16:]
-
-    stream(NEAR_REST // NEAR_STEP, near_first, near_second)
-    near_parts[NEAR_REST] = jnp.zeros((16, 128), F32)
-
     for copy in far_halo:
         copy.wait()
     prepare_far(0, s_low, l_low)
@@ -473,6 +447,29 @@
 
     stream(leaves // FAR_STEP, far_first, far_second)
 
+    for copy in near_halo:
+        copy.wait()
+    prepare_near(0, p_low, c_low)
+    prepare_near(2, p_high, c_high)
+
+    def near_code(i, k):
+        code = near_codes[0, i * NEAR_STEP + k]
+        return code // 1024, lax.rem(code, 1024)
+
+    def near_first(i):
+        for k in range(NEAR_STEP):
+            t, s = near_code(i, k)
+            near_blocks[k] = kernel_block(near_targets[t], near_sources[s])
+
+    def near_second(i):
+        for k in range(NEAR_STEP):
+            _, s = near_code(i, k)
+            sums = dot(near_weights[s], near_blocks[k], NT)
+            near_parts[i * NEAR_STEP + k] = sums[:16] + sums[16:]
+
+    stream(NEAR_REST // NEAR_STEP, near_first, near_second)
+    near_parts[NEAR_REST] = jnp.zeros((16, 128), F32)
+
     for copy in group_copies:
         copy.wait()
     loads[6].wait()
@@ -508,30 +505,33 @@
         in_pairs(nodes, n_narrow),
         marked(node_links, g * n_narrow, n_narrow),
     )
-    field_halves = jnp.concatenate(halves(node_fields), axis=0)
-
-    loads[7].wait()
-    loads[8].wait()
-
-    def downward(i, carry):
-        at = pl.ds(pl.multiple_of(i * 128, 128), 128)
-        product = dot(field_halves, beside(downward_own[:, at]), NN)
-        fields = product[:16, :128] + product[16:, :128] + product[:16, 128:] + couple[:, at]
-        low = lane((16, 128)) < 64
-        lefts = [jnp.where(low, fields, 0.0), jnp.where(low, 0.0, fields)]
+    fields[...] = node_fields
+
+    def collect(leaf, carry):
+        span = pl.ds(pl.multiple_of(leaf * 128, 128), 128)
+        value = near[:, span]
+        for slot in range(1, near_list.shape[0]):
+            value = value + near_parts[near_places[slot, leaf]]
+        near[:, span] = value
+        return carry
+
+    lax.fori_loop(0, leaves, collect, 0, unroll=8)
+
+
+def finish(fields, near, couple, leaf_downward, basis, out):
+    field_halves = jnp.concatenate(halves(fields[...]), axis=0)
+    low = lane((16, 128)) < 64
+    for i in range(basis.shape[0]):
+        at = slice(128 * i, 128 * (i + 1))
+        product = dot(field_halves, beside(leaf_downward[:, at]), NN)
+        leaf = product[:16, :128] + product[16:, :128] + product[:16, 128:] + couple[:, at]
+        lefts = [jnp.where(low, leaf, 0.0), jnp.where(low, 0.0, leaf)]
         left = jnp.concatenate([h for x in lefts for h in halves(x)], axis=0)
-        product = dot(left, beside(basis_down[i]), NN)
+        product = dot(left, beside(basis[i]), NN)
         for k in range(2):
-            leaf = 2 * i + k
             rows = product[32 * k : 32 * (k + 1)]
-            value = rows[:16, :128] + rows[16:, :128] + rows[:16, 128:]
-            for slot in range(1, near_list.shape[0]):
-                value = value + near_parts[near_places[slot, leaf]]
-            span = pl.ds(pl.multiple_of(leaf * 128, 128), 128)
-            far_out[:, span] = value
-        return carry
-
-    lax.fori_loop(0, leaves // 2, downward, 0, unroll=4)
+            span = slice(256 * i + 128 * k, 256 * i + 128 * (k + 1))
+            out[:, span] = near[:, span] + (rows[:16, :128] + rows[16:, :128] + rows[:16, 128:])
 
 
 def on_device(
@@ -569,20 +569,22 @@
     def sems(count):
         return pltpu.SemaphoreType.DMA((count,))
 
-    near, far = pl.pallas_call(
+    near, couple, fields = pl.pallas_call(
         fused,
-        out_shape=[jax.ShapeDtypeStruct(charges.shape, F32)] * 2,
-        in_specs=[vmem] * 2 + [smem] * 2 + [anywhere] * 9 + [vmem] * 2,
-        out_specs=[vmem] * 2,
+        out_shape=[
+            jax.ShapeDtypeStruct(charges.shape, F32),
+            jax.ShapeDtypeStruct((16, leaf_skel.shape[1]), F32),
+            jax.ShapeDtypeStruct((16, rank), F32),
+        ],
+        in_specs=[vmem] * 2 + [smem] * 2 + [anywhere] * 7 + [vmem] * 2,
+        out_specs=[vmem] * 3,
         scratch_shapes=[
             *[f32(*points.shape)] * 3,
             *[f32(*charges.shape)] * 3,
             *[f32(*leaf_skel.shape)] * 3,
             *[f32(16, leaf_skel.shape[1])] * 3,
             f32(*paired),
-            f32(*paired),
             f32(*leaf_upward.shape),
-            f32(*leaf_downward.shape),
             f32(64, 64 * n_narrow),
             f32(6, 64 * n_narrow),
             f32(n_narrow, *table),
@@ -598,14 +600,13 @@
             bf16(tables, 32, 256),
             bf16(leaves, 64, 48),
             bf16(4 * FAR_STEP, 64, 256),
-            f32(16, leaf_skel.shape[1]),
             pltpu.VMEM((1, 256), jnp.int32),
             pltpu.VMEM((8, 128), jnp.int32),
             pltpu.VMEM((8, 128), jnp.int32),
             pltpu.SMEM((1, 256), jnp.int32),
             pltpu.SMEM((8, 128), jnp.int32),
             pltpu.SMEM((8, 128), jnp.int32),
-            sems(9),
+            sems(7),
             sems(3),
             sems(8),
             sems(8),
@@ -630,12 +631,28 @@
         leaf_upward,
         node_upward,
         node_skel,
-        target_basis.reshape(paired),
-        leaf_downward,
         node_downward,
         group_skel,
     )
-    return near + far
+    steps = FINISH_STEPS
+
+    def columns(rows, total):
+        return pl.BlockSpec((rows, total // steps), lambda i: (0, i))
+
+    return pl.pallas_call(
+        finish,
+        grid=(steps,),
+        out_shape=jax.ShapeDtypeStruct(charges.shape, F32),
+        in_specs=[
+            pl.BlockSpec(fields.shape, lambda i: (0, 0)),
+            columns(*near.shape),
+            columns(*couple.shape),
+            columns(*leaf_downward.shape),
+            pl.BlockSpec((paired[0] // steps, *paired[1:]), lambda i: (i, 0, 0)),
+        ],
+        out_specs=columns(*near.shape),
+        name="finish",
+    )(fields, near, couple, leaf_downward, target_basis.reshape(paired))
 
 
 def solution(mesh):

time: 48.8 us -> 47.7 us (0.977); the launches traced: 47.9 us -> 47.5 us
  other arithmetic: 2.05 us -> 0 us
  Pallas kernels: 45.8 us -> 47.5 us
    pallas_call x0 -> x1, Pallas kernels: none -> 5.42 us  [on_device(): pl.pallas_call(finish, grid=(steps,), out_shape=jax.ShapeDtypeStruct(char...]
    pallas_call x1, Pallas kernels: 45.8 us -> 42 us  [on_device(): pl.pallas_call(fused, out_shape=[jax.ShapeDtypeStruct(charges.shape, F32)...]
    add x1 -> x0, other arithmetic: 2.05 us -> none  [on_device(): return near + far]
where the time goes in v4:
time: 47.7 us; the launch traced here: 47.5 us
  Pallas kernels  47.5 us (100%)
    pallas_call x1, Pallas kernels, on_device(): pl.pallas_call(fused, out_shape=[jax.ShapeDtypeStruct(charges.shape, F32)...  42 us
    pallas_call x1, Pallas kernels, on_device(): pl.pallas_call(finish, grid=(steps,), out_shape=jax.ShapeDtypeStruct(char...  5.42 us

profile of v4, /device:TPU:0, one launch (start us, length us, event | category | flops | bytes accessed | tf_op | source)
XLA Modules:
  0.0 47.5 jit_solution(7811496087780104572)
XLA Ops:
  0.0 42.0 %fused.1 = (f32[16,8192]{1,0:T(8,128)}, f32[16,4096]{1,0:T(8,128)}, f32[16,64]{1,0:T(8,128)}) custom-call(s32[8,64]{1,0:T(8,128)} %bitcast.6, s32[8,64]{1,0:T(8,128)} %bitcast.7, s32[1,4]{1,0:T(1,128)} %node_links.1, s32[1,8]{1,0:T(1,128)} %group_links.1, f32[6,8192]{1,0:T(8,128)} %points.1, f32[16,8192]{1,0:T(8,128)} %charges.1, f32[6,4096]{1,0:T(8,128)} %leaf_skel.1, ...), custom_call_target="tpu_custom_call" | custom-call | tf_op jit(solution)/shard_map/fused/pallas_call | solution.py:572
  42.1 5.4 %finish.1 = f32[16,8192]{1,0:T(8,128)} custom-call(f32[16,64]{1,0:T(8,128)} %get-tuple-element.8.fields, f32[16,8192]{1,0:T(8,128)} %get-tuple-element.9.near, f32[16,4096]{1,0:T(8,128)} %get-tuple-element.10.couple, f32[64,4096]{1,0:T(8,128)} %leaf_downward.1, f32[32,128,128]{2,1,0:T(8,128)} %bitcast.4), custom_call_target="tpu_custom_call" | custom-call | tf_op jit(solution)/shard_map/finish/pallas_call | solution.py:642

commit v5 on v4

--- a/solution.py
+++ b/solution.py
@@ -198,6 +198,11 @@
     far_weights,
     far_targets,
     far_blocks,
+    near_list_v,
+    leaf_links_v,
+    group_skel_v,
+    node_downward_v,
+    couple_v,
     near_codes_v,
     near_places_v,
     far_codes_v,
@@ -234,9 +239,13 @@
             (source_basis, basis_up),
             (leaf_upward, upward_own),
             (points, p_own),
+            (near_list, near_list_v),
+            (leaf_links, leaf_links_v),
             (leaf_skel, s_own),
             (node_upward.at[:, group_span], group_upward),
             (node_skel.at[:, group_span], nodes_skel),
+            (group_skel, group_skel_v),
+            (node_downward, node_downward_v),
         )
     ):
         copy = pltpu.make_async_copy(source, target, load_sem.at[k])
@@ -254,7 +263,6 @@
         pl.semaphore_signal(
             barrier, inc=1, device_id=(lax.rem(g + step, n_wide), n), device_id_type=MESH
         )
-    pl.semaphore_wait(barrier, n_narrow + n_wide)
 
     def send(source, low, high, at):
         copies = []
@@ -271,19 +279,6 @@
             copies.append(copy)
         return copies
 
-    near_halo = send(points, p_low, p_high, 0)
-    far_halo = send(leaf_skel, s_low, s_high, 2)
-
-    codes, places, far = lists(near_list[...], leaf_links[...], first_leaf)
-    near_codes_v[...], near_places_v[...], far_codes_v[...] = codes, places, far
-    list_copies = []
-    for k, (source, target) in enumerate(
-        ((near_codes_v, near_codes), (near_places_v, near_places), (far_codes_v, far_codes))
-    ):
-        copy = pltpu.make_async_copy(source, target, list_sem.at[k])
-        copy.start()
-        list_copies.append(copy)
-
     for copy in loads[:3]:
         copy.wait()
 
@@ -305,6 +300,76 @@
     own = total[:16] + total[16:]
     node_mine[...] = jnp.concatenate([own, jnp.zeros_like(own)], axis=1)
 
+    zero_rows = [jnp.zeros((8, 128), F32)] * 6
+    for table in (near_sources, far_sources):
+        parts = [source_parts(v) for v in source_values(zero_rows)]
+        table[spare] = jnp.concatenate(parts, axis=1)
+    for table in (near_weights, far_weights):
+        table[spare] = jnp.zeros(table.shape[1:], BF16)
+
+    def prepare_near(side, points_ref, charges_ref):
+        def body(i, carry):
+            start = pl.multiple_of(i * 128, 128)
+            rows = source_tile(points_ref, start, 128)
+            parts = [source_parts(v) for v in source_values(rows)]
+            near_sources[side * leaves + i] = jnp.concatenate(parts, axis=1)
+            near_weights[side * leaves + i] = twice(charges_ref[:, pl.ds(start, 128)])
+            if side == 1:
+                near_targets[i] = target_parts(rows)
+            return carry
+
+        lax.fori_loop(0, leaves, body, 0, unroll=4)
+
+    def both_halves(x):
+        low = lane(x.shape) < 64
+        turned = pltpu.roll(x, 64, 1)
+        return jnp.where(low, x, turned), jnp.where(low, turned, x)
+
+    def prepare_far(side, points_ref, charges_ref):
+        def body(i, carry):
+            start = pl.multiple_of(i * 128, 128)
+            rows = source_tile(points_ref, start, 128)
+            split = [both_halves(v) for v in source_values(rows)]
+            weights = both_halves(charges_ref[:, pl.ds(start, 128)])
+            for k in range(2):
+                parts = [source_parts(v[k]) for v in split]
+                far_sources[side * leaves + 2 * i + k] = jnp.concatenate(parts, axis=1)
+                far_weights[side * leaves + 2 * i + k] = twice(weights[k])
+            if side == 1:
+                targets = target_parts(rows)
+                far_targets[2 * i] = targets[:64]
+                far_targets[2 * i + 1] = targets[64:]
+            return carry
+
+        lax.fori_loop(0, leaves // 2, body, 0, unroll=4)
+
+    def stream(count, first, second):
+        first(0)
+
+        def body(i, carry):
+            second(i - 1)
+            first(i)
+            return carry
+
+        lax.fori_loop(1, count, body, 0)
+        second(count - 1)
+
+    loads[3].wait()
+    prepare_near(1, p_own, c_own)
+
+    for copy in loads[4:6]:
+        copy.wait()
+    codes, places, far = lists(near_list_v[...], leaf_links_v[...], first_leaf)
+    near_codes_v[...], near_places_v[...], far_codes_v[...] = codes, places, far
+    list_copies = []
+    for k, (source, target) in enumerate(
+        ((near_codes_v, near_codes), (near_places_v, near_places), (far_codes_v, far_codes))
+    ):
+        copy = pltpu.make_async_copy(source, target, list_sem.at[k])
+        copy.start()
+        list_copies.append(copy)
+
+    pl.semaphore_wait(barrier, n_narrow + n_wide)
     def gather(count, mine, table, device_of, place, send_sems, recv_sems):
         copies = []
         for step in range(1, count):
@@ -324,65 +389,9 @@
     node_copies = gather(
         n_narrow, node_mine, nodes, lambda step: (g, lax.rem(n + step, n_narrow)), n, node_send, node_recv
     )
-    far_halo += send(l_own, l_low, l_high, 3)
-    near_halo += send(charges, c_low, c_high, 1)
-
-    zero_rows = [jnp.zeros((8, 128), F32)] * 6
-    for table in (near_sources, far_sources):
-        parts = [source_parts(v) for v in source_values(zero_rows)]
-        table[spare] = jnp.concatenate(parts, axis=1)
-    for table in (near_weights, far_weights):
-        table[spare] = jnp.zeros(table.shape[1:], BF16)
-
-    def prepare_near(side, points_ref, charges_ref):
-        def body(i, carry):
-            start = pl.multiple_of(i * 128, 128)
-            rows = source_tile(points_ref, start, 128)
-            parts = [source_parts(v) for v in source_values(rows)]
-            near_sources[side * leaves + i] = jnp.concatenate(parts, axis=1)
-            near_weights[side * leaves + i] = twice(charges_ref[:, pl.ds(start, 128)])
-            if side == 1:
-                near_targets[i] = target_parts(rows)
-            return carry
-
-        lax.fori_loop(0, leaves, body, 0, unroll=4)
-
-    def both_halves(x):
-        low = lane(x.shape) < 64
-        turned = pltpu.roll(x, 64, 1)
-        return jnp.where(low, x, turned), jnp.where(low, turned, x)
-
-    def prepare_far(side, points_ref, charges_ref):
-        def body(i, carry):
-            start = pl.multiple_of(i * 128, 128)
-            rows = source_tile(points_ref, start, 128)
-            split = [both_halves(v) for v in source_values(rows)]
-            weights = both_halves(charges_ref[:, pl.ds(start, 128)])
-            for k in range(2):
-                parts = [source_parts(v[k]) for v in split]
-                far_sources[side * leaves + 2 * i + k] = jnp.concatenate(parts, axis=1)
-                far_weights[side * leaves + 2 * i + k] = twice(weights[k])
-            if side == 1:
-                targets = target_parts(rows)
-                far_targets[2 * i] = targets[:64]
-                far_targets[2 * i + 1] = targets[64:]
-            return carry
-
-        lax.fori_loop(0, leaves // 2, body, 0, unroll=4)
-
-    def stream(count, first, second):
-        first(0)
-
-        def body(i, carry):
-            second(i - 1)
-            first(i)
-            return carry
-
-        lax.fori_loop(1, count, body, 0)
-        second(count - 1)
-
-    loads[3].wait()
-    prepare_near(1, p_own, c_own)
+    far_halo = send(leaf_skel, s_low, s_high, 2) + send(l_own, l_low, l_high, 3)
+    near_halo = send(points, p_low, p_high, 0) + send(charges, c_low, c_high, 1)
+
 
     def self_first(i):
         for k in range(NEAR_STEP):
@@ -397,12 +406,12 @@
 
     stream(leaves // NEAR_STEP, self_first, self_second)
 
-    loads[4].wait()
+    loads[6].wait()
     prepare_far(1, s_own, l_own)
 
     for copy in node_copies:
         copy.wait()
-    loads[5].wait()
+    loads[7].wait()
     group = dot(
         twice(jnp.concatenate(in_pairs(nodes, n_narrow), axis=1)), beside(group_upward[...]), NT
     )
@@ -443,9 +452,11 @@
         sums = [x[:16] + x[16:] for x in sums]
         for k in range(0, FAR_STEP, 2):
             at = pl.ds(pl.multiple_of((FAR_STEP * i + k) * 64, 128), 128)
-            couple[:, at] = jnp.concatenate(sums[k : k + 2], axis=1)
+            couple_v[:, at] = jnp.concatenate(sums[k : k + 2], axis=1)
 
     stream(leaves // FAR_STEP, far_first, far_second)
+    couple_store = pltpu.make_async_copy(couple_v, couple, load_sem.at[11])
+    couple_store.start()
 
     for copy in near_halo:
         copy.wait()
@@ -472,7 +483,8 @@
 
     for copy in group_copies:
         copy.wait()
-    loads[6].wait()
+    for copy in loads[8:11]:
+        copy.wait()
 
     def half_of(skel, start, which):
         tile = source_tile(skel, pl.multiple_of(start, 128), 128)
@@ -494,12 +506,12 @@
         return sums[:16] + sums[16:]
 
     group_fields = small(
-        half_of(group_skel, (g // 2) * 128, lax.rem(g, 2)),
-        group_skel[...],
+        half_of(group_skel_v, (g // 2) * 128, lax.rem(g, 2)),
+        group_skel_v[...],
         in_pairs(groups, n_wide),
         marked(group_links, 0, n_wide),
     )
-    node_fields = dot(group_fields, node_downward[...], NN, HIGH) + small(
+    node_fields = dot(group_fields, node_downward_v[...], NN, HIGH) + small(
         half_of(nodes_skel, (n // 2) * 128, lax.rem(n, 2)),
         nodes_skel[...],
         in_pairs(nodes, n_narrow),
@@ -516,6 +528,7 @@
         return carry
 
     lax.fori_loop(0, leaves, collect, 0, unroll=8)
+    couple_store.wait()
 
 
 def finish(fields, near, couple, leaf_downward, basis, out):
@@ -576,8 +589,8 @@
             jax.ShapeDtypeStruct((16, leaf_skel.shape[1]), F32),
             jax.ShapeDtypeStruct((16, rank), F32),
         ],
-        in_specs=[vmem] * 2 + [smem] * 2 + [anywhere] * 7 + [vmem] * 2,
-        out_specs=[vmem] * 3,
+        in_specs=[anywhere] * 2 + [smem] * 2 + [anywhere] * 9,
+        out_specs=[vmem, anywhere, vmem],
         scratch_shapes=[
             *[f32(*points.shape)] * 3,
             *[f32(*charges.shape)] * 3,
@@ -600,13 +613,18 @@
             bf16(tables, 32, 256),
             bf16(leaves, 64, 48),
             bf16(4 * FAR_STEP, 64, 256),
+            pltpu.VMEM(near_list.shape[::-1], jnp.int32),
+            pltpu.VMEM(leaf_links.shape[::-1], jnp.int32),
+            f32(*group_skel.shape),
+            f32(*node_downward.shape),
+            f32(16, leaf_skel.shape[1]),
             pltpu.VMEM((1, 256), jnp.int32),
             pltpu.VMEM((8, 128), jnp.int32),
             pltpu.VMEM((8, 128), jnp.int32),
             pltpu.SMEM((1, 256), jnp.int32),
             pltpu.SMEM((8, 128), jnp.int32),
             pltpu.SMEM((8, 128), jnp.int32),
-            sems(7),
+            sems(12),
             sems(3),
             sems(8),
             sems(8),

time: 47.7 us -> 51.2 us (1.073)
  Pallas kernels: 47.5 us -> 51 us
    pallas_call x1, Pallas kernels: 42 us -> 45.6 us  [on_device(): pl.pallas_call(fused, out_shape=[jax.ShapeDtypeStruct(charges.shape, F32)...]
where the time goes in v5:
time: 51.2 us; the launch traced here: 51 us
  Pallas kernels  51 us (100%)
    pallas_call x1, Pallas kernels, on_device(): pl.pallas_call(fused, out_shape=[jax.ShapeDtypeStruct(charges.shape, F32)...  45.6 us
    pallas_call x1, Pallas kernels, on_device(): pl.pallas_call(finish, grid=(steps,), out_shape=jax.ShapeDtypeStruct(char...  5.42 us

profile of v5, /device:TPU:0, one launch (start us, length us, event | category | flops | bytes accessed | tf_op | source)
XLA Modules:
  0.0 51.0 jit_solution(15051545751603146461)
XLA Ops:
  0.0 45.6 %fused.1 = (f32[16,8192]{1,0:T(8,128)}, f32[16,4096]{1,0:T(8,128)}, f32[16,64]{1,0:T(8,128)}) custom-call(s32[8,64]{1,0:T(8,128)} %bitcast.6, s32[8,64]{1,0:T(8,128)} %bitcast.7, s32[1,4]{1,0:T(1,128)} %node_links.1, s32[1,8]{1,0:T(1,128)} %group_links.1, f32[6,8192]{1,0:T(8,128)} %points.1, f32[16,8192]{1,0:T(8,128)} %charges.1, f32[6,4096]{1,0:T(8,128)} %leaf_skel.1, ...), custom_call_target="tpu_custom_call" | custom-call | tf_op jit(solution)/shard_map/fused/pallas_call | solution.py:585
  45.6 5.4 %finish.1 = f32[16,8192]{1,0:T(8,128)} custom-call(f32[16,64]{1,0:T(8,128)} %get-tuple-element.8.fields, f32[16,8192]{1,0:T(8,128)} %get-tuple-element.9.near, f32[16,4096]{1,0:T(8,128)} %get-tuple-element.10.couple, f32[64,4096]{1,0:T(8,128)} %leaf_downward.1, f32[32,128,128]{2,1,0:T(8,128)} %bitcast.4), custom_call_target="tpu_custom_call" | custom-call | tf_op jit(solution)/shard_map/finish/pallas_call | solution.py:660

commit v6 on v5

--- a/solution.py
+++ b/solution.py
@@ -264,6 +264,8 @@
             barrier, inc=1, device_id=(lax.rem(g + step, n_wide), n), device_id_type=MESH
         )
 
+    pl.semaphore_wait(barrier, n_narrow + n_wide)
+
     def send(source, low, high, at):
         copies = []
         for target, device, k in ((low, after, 2 * at), (high, before, 2 * at + 1)):
@@ -279,6 +281,9 @@
             copies.append(copy)
         return copies
 
+    far_halo = send(leaf_skel, s_low, s_high, 2)
+    near_halo = send(points, p_low, p_high, 0)
+
     for copy in loads[:3]:
         copy.wait()
 
@@ -296,9 +301,30 @@
         l_own[:, at] = values
         return total + dot(twice(values), beside(upward_own[:, at]), NT)
 
-    total = lax.fori_loop(0, leaves // 2, upward, jnp.zeros((32, 64), F32), unroll=8)
+    total = lax.fori_loop(0, leaves // 2, upward, jnp.zeros((32, 64), F32), unroll=16)
     own = total[:16] + total[16:]
     node_mine[...] = jnp.concatenate([own, jnp.zeros_like(own)], axis=1)
+
+    def gather(count, mine, table, device_of, place, send_sems, recv_sems):
+        copies = []
+        for step in range(1, count):
+            copy = pltpu.make_async_remote_copy(
+                src_ref=mine,
+                dst_ref=table.at[place],
+                send_sem=send_sems.at[step],
+                recv_sem=recv_sems.at[step],
+                device_id=device_of(step),
+                device_id_type=MESH,
+            )
+            copy.start()
+            copies.append(copy)
+        table[place] = mine[...]
+        return copies
+
+    node_copies = gather(
+        n_narrow, node_mine, nodes, lambda step: (g, lax.rem(n + step, n_narrow)), n, node_send, node_recv
+    )
+    far_halo += send(l_own, l_low, l_high, 3)
 
     zero_rows = [jnp.zeros((8, 128), F32)] * 6
     for table in (near_sources, far_sources):
@@ -318,7 +344,7 @@
                 near_targets[i] = target_parts(rows)
             return carry
 
-        lax.fori_loop(0, leaves, body, 0, unroll=4)
+        lax.fori_loop(0, leaves, body, 0, unroll=8)
 
     def both_halves(x):
         low = lane(x.shape) < 64
@@ -341,7 +367,7 @@
                 far_targets[2 * i + 1] = targets[64:]
             return carry
 
-        lax.fori_loop(0, leaves // 2, body, 0, unroll=4)
+        lax.fori_loop(0, leaves // 2, body, 0, unroll=8)
 
     def stream(count, first, second):
         first(0)
@@ -356,6 +382,7 @@
 
     loads[3].wait()
     prepare_near(1, p_own, c_own)
+    near_halo += send(charges, c_low, c_high, 1)
 
     for copy in loads[4:6]:
         copy.wait()
@@ -368,30 +395,6 @@
         copy = pltpu.make_async_copy(source, target, list_sem.at[k])
         copy.start()
         list_copies.append(copy)
-
-    pl.semaphore_wait(barrier, n_narrow + n_wide)
-    def gather(count, mine, table, device_of, place, send_sems, recv_sems):
-        copies = []
-        for step in range(1, count):
-            copy = pltpu.make_async_remote_copy(
-                src_ref=mine,
-                dst_ref=table.at[place],
-                send_sem=send_sems.at[step],
-                recv_sem=recv_sems.at[step],
-                device_id=device_of(step),
-                device_id_type=MESH,
-            )
-            copy.start()
-            copies.append(copy)
-        table[place] = mine[...]
-        return copies
-
-    node_copies = gather(
-        n_narrow, node_mine, nodes, lambda step: (g, lax.rem(n + step, n_narrow)), n, node_send, node_recv
-    )
-    far_halo = send(leaf_skel, s_low, s_high, 2) + send(l_own, l_low, l_high, 3)
-    near_halo = send(points, p_low, p_high, 0) + send(charges, c_low, c_high, 1)
-
 
     def self_first(i):
         for k in range(NEAR_STEP):

time: 51.2 us -> 47.2 us (0.922)
  Pallas kernels: 51 us -> 47 us
    pallas_call x1, Pallas kernels: 45.6 us -> 41.6 us  [on_device(): pl.pallas_call(fused, out_shape=[jax.ShapeDtypeStruct(charges.shape, F32)...]
where the time goes in v6:
time: 47.2 us; the launch traced here: 47 us
  Pallas kernels  47 us (100%)
    pallas_call x1, Pallas kernels, on_device(): pl.pallas_call(fused, out_shape=[jax.ShapeDtypeStruct(charges.shape, F32)...  41.6 us
    pallas_call x1, Pallas kernels, on_device(): pl.pallas_call(finish, grid=(steps,), out_shape=jax.ShapeDtypeStruct(char...  5.42 us

profile of v6, /device:TPU:0, one launch (start us, length us, event | category | flops | bytes accessed | tf_op | source)
XLA Modules:
  0.0 47.0 jit_solution(640677125777230225)
XLA Ops:
  0.0 41.6 %fused.1 = (f32[16,8192]{1,0:T(8,128)}, f32[16,4096]{1,0:T(8,128)}, f32[16,64]{1,0:T(8,128)}) custom-call(s32[8,64]{1,0:T(8,128)} %bitcast.6, s32[8,64]{1,0:T(8,128)} %bitcast.7, s32[1,4]{1,0:T(1,128)} %node_links.1, s32[1,8]{1,0:T(1,128)} %group_links.1, f32[6,8192]{1,0:T(8,128)} %points.1, f32[16,8192]{1,0:T(8,128)} %charges.1, f32[6,4096]{1,0:T(8,128)} %leaf_skel.1, ...), custom_call_target="tpu_custom_call" | custom-call | tf_op jit(solution)/shard_map/fused/pallas_call | solution.py:588
  41.6 5.4 %finish.1 = f32[16,8192]{1,0:T(8,128)} custom-call(f32[16,64]{1,0:T(8,128)} %get-tuple-element.8.fields, f32[16,8192]{1,0:T(8,128)} %get-tuple-element.9.near, f32[16,4096]{1,0:T(8,128)} %get-tuple-element.10.couple, f32[64,4096]{1,0:T(8,128)} %leaf_downward.1, f32[32,128,128]{2,1,0:T(8,128)} %bitcast.4), custom_call_target="tpu_custom_call" | custom-call | tf_op jit(solution)/shard_map/finish/pallas_call | solution.py:663

commit v7 on v6

--- a/solution.py
+++ b/solution.py
@@ -16,7 +16,8 @@
 NN = (((1,), (0,)), ((), ()))
 NEAR_REST = 288 - 64
 NEAR_STEP = 32
-FAR_STEP = 8
+REST_STEP = 56
+FAR_STEP = 16
 FINISH_STEPS = 4
 VMEM_LIMIT = 56 * 2**20
 
@@ -467,21 +468,21 @@
     prepare_near(2, p_high, c_high)
 
     def near_code(i, k):
-        code = near_codes[0, i * NEAR_STEP + k]
+        code = near_codes[0, i * REST_STEP + k]
         return code // 1024, lax.rem(code, 1024)
 
     def near_first(i):
-        for k in range(NEAR_STEP):
+        for k in range(REST_STEP):
             t, s = near_code(i, k)
             near_blocks[k] = kernel_block(near_targets[t], near_sources[s])
 
     def near_second(i):
-        for k in range(NEAR_STEP):
+        for k in range(REST_STEP):
             _, s = near_code(i, k)
             sums = dot(near_weights[s], near_blocks[k], NT)
-            near_parts[i * NEAR_STEP + k] = sums[:16] + sums[16:]
-
-    stream(NEAR_REST // NEAR_STEP, near_first, near_second)
+            near_parts[i * REST_STEP + k] = sums[:16] + sums[16:]
+
+    stream(NEAR_REST // REST_STEP, near_first, near_second)
     near_parts[NEAR_REST] = jnp.zeros((16, 128), F32)
 
     for copy in group_copies:
@@ -610,7 +611,7 @@
             bf16(tables, 48, 256),
             bf16(tables, 32, 256),
             bf16(leaves, 128, 48),
-            bf16(NEAR_STEP, 128, 256),
+            bf16(REST_STEP, 128, 256),
             f32(NEAR_REST + 1, *table),
             bf16(tables, 48, 256),
             bf16(tables, 32, 256),

time: 47.2 us -> 46.5 us (0.985)
  Pallas kernels: 47 us -> 46.4 us
    pallas_call x1, Pallas kernels: 41.6 us -> 40.9 us  [on_device(): pl.pallas_call(fused, out_shape=[jax.ShapeDtypeStruct(charges.shape, F32)...]
where the time goes in v7:
time: 46.5 us; the launch traced here: 46.4 us
  Pallas kernels  46.4 us (100%)
    pallas_call x1, Pallas kernels, on_device(): pl.pallas_call(fused, out_shape=[jax.ShapeDtypeStruct(charges.shape, F32)...  40.9 us
    pallas_call x1, Pallas kernels, on_device(): pl.pallas_call(finish, grid=(steps,), out_shape=jax.ShapeDtypeStruct(char...  5.42 us

profile of v7, /device:TPU:0, one launch (start us, length us, event | category | flops | bytes accessed | tf_op | source)
XLA Modules:
  0.0 46.4 jit_solution(9902829115835359041)
XLA Ops:
  0.0 40.9 %fused.1 = (f32[16,8192]{1,0:T(8,128)}, f32[16,4096]{1,0:T(8,128)}, f32[16,64]{1,0:T(8,128)}) custom-call(s32[8,64]{1,0:T(8,128)} %bitcast.6, s32[8,64]{1,0:T(8,128)} %bitcast.7, s32[1,4]{1,0:T(1,128)} %node_links.1, s32[1,8]{1,0:T(1,128)} %group_links.1, f32[6,8192]{1,0:T(8,128)} %points.1, f32[16,8192]{1,0:T(8,128)} %charges.1, f32[6,4096]{1,0:T(8,128)} %leaf_skel.1, ...), custom_call_target="tpu_custom_call" | custom-call | tf_op jit(solution)/shard_map/fused/pallas_call | solution.py:589
  40.9 5.4 %finish.1 = f32[16,8192]{1,0:T(8,128)} custom-call(f32[16,64]{1,0:T(8,128)} %get-tuple-element.8.fields, f32[16,8192]{1,0:T(8,128)} %get-tuple-element.9.near, f32[16,4096]{1,0:T(8,128)} %get-tuple-element.10.couple, f32[64,4096]{1,0:T(8,128)} %leaf_downward.1, f32[32,128,128]{2,1,0:T(8,128)} %bitcast.4), custom_call_target="tpu_custom_call" | custom-call | tf_op jit(solution)/shard_map/finish/pallas_call | solution.py:664
